TPU v7x, 256 devices: a whole 4x4x8 slice. The times are simulated.
256 devices in a mesh: seq: 128 (over x, z, y), vocab: 2 (over core).
Axes of the slice: x: 4, y: 4, z: 8, core: 2. Of those that a mesh axis runs over, the one named last changes fastest.
Arguments:
- frames: bfloat16 [65536, 1280], P('seq', 'vocab'), may hold values from -6 to 6
- conv_weight: bfloat16 [31, 1280], P(None, 'vocab'), may hold values from -1 to 1
- proj_weight: bfloat16 [1280, 3584], P('seq', 'vocab'), may hold values from -0.15625 to 0.15625
- table: bfloat16 [152064, 3584], P('seq', 'vocab'), may hold values from -6 to 6
- audio_pos: int32 [16384], P('seq'), may hold values from 0 to 32767, as said below
- token_ids: int32 [32768], P('seq'), may hold values from 0 to 152063, as said below
- cotangent: bfloat16 [32768, 3584], P('seq', 'vocab'), may hold values from -6 to 6
Outputs:
- llm_input: bfloat16 [32768, 3584], P('seq', 'vocab')
- grad_table: bfloat16 [152064, 3584], P('seq', 'vocab')
Inputs may be any that keep to these rules, and one draw needn't show every extreme that they name: `audio_pos`: the entries are distinct; with the slots not named they cover all slots once. The 128 rows of one aligned block of 128 rows take consecutive slots in order. A row held by seq device s (rows s * 128 to (s + 1) * 128 - 1) goes to a slot of s * 256 to (s + 2) * 256 - 1. For every seq device s but the last, its last held row goes to a slot of seq device s + 1. `token_ids`: seq device s holds vocabulary rows s * 1188 to (s + 1) * 1188 - 1 and slots s * 256 to (s + 1) * 256 - 1. Among the slots of one seq device at most 2 ids fall in the rows of one seq device, and in every such block of slots exactly 2 fall in the rows of some seq device.
All inputs are finite; a program needn't handle non-finite values.
Results may differ from a plain program's by a relative error of at most 0.0023.
Values may be sent and summed in bfloat16 or wider, within the bound.
A program may use at most 128 MiB of HBM per device.

v0:
```python
import jax
import jax.numpy as jnp
from jax import lax
from jax.sharding import PartitionSpec as P

POOL = 4


def extended(array, sides, width):
    for axis, dim in sides:
        size, length = (lax.axis_size(axis), array.shape[dim])
        up = [(i, (i + 1) % size) for i in range(size - 1)]
        down = [(j, i) for i, j in up]
        last = lax.slice_in_dim(array, length - width, length, axis=dim)
        first = lax.slice_in_dim(array, 0, width, axis=dim)
        before = lax.ppermute(last, axis, up)
        after = lax.ppermute(first, axis, down)
        array = jnp.concatenate([before, array, after], axis=dim)
    return array


def from_behind(array, axis, by):
    size = lax.axis_size(axis)
    pairs = [(i, i + by) for i in range(size) if 0 <= i + by < size]
    return lax.ppermute(array, axis, pairs)


def depthwise(padded, conv_weight, frames_count):
    running = jnp.zeros((frames_count, conv_weight.shape[1]), jnp.float32)
    for tap_index in range(conv_weight.shape[0]):
        running = running + padded[tap_index : tap_index + frames_count].astype(
            jnp.float32
        ) * conv_weight[tap_index].astype(jnp.float32)
    return running


def project(source, proj_weight):
    return jnp.dot(
        source,
        lax.all_gather(proj_weight, "seq", axis=0, tiled=True),
        preferred_element_type=jnp.float32,
    )


def shards(frames, conv_weight, proj_weight, table, audio_pos, token_ids, cotangent):
    frames_count = frames.shape[0]
    rim_width = (conv_weight.shape[0] - 1) // 2
    padded = extended(frames, (("seq", 0),), rim_width)
    filtered = depthwise(padded, conv_weight, frames_count)
    activated = frames.astype(jnp.float32) + jax.nn.silu(filtered)
    pool_rows = frames_count // POOL
    pooled = (
        activated.reshape(pool_rows, POOL, activated.shape[1]).mean(axis=1).astype(jnp.bfloat16)
    )
    marked = audio_pos + 1
    gathered = lax.all_gather(pooled, "vocab", axis=1, tiled=True)
    own_rows = project(gathered, proj_weight).astype(jnp.bfloat16)
    earlier_rows, earlier_marked = from_behind((own_rows, marked), "seq", 1)
    slot_count = cotangent.shape[0]
    feature_count = cotangent.shape[1]
    slot_start = lax.axis_index("seq") * slot_count
    own_local = audio_pos - slot_start
    own_index = jnp.where(own_local < slot_count, own_local, slot_count)
    earlier_local = earlier_marked - 1 - slot_start
    earlier_index = jnp.where(
        (earlier_marked > 0) & (earlier_local >= 0), earlier_local, slot_count
    )
    targets = jnp.concatenate([own_index, earlier_index])
    arriving = jnp.concatenate([own_rows, earlier_rows], axis=0)
    audio_part = (
        jnp.zeros((slot_count, feature_count), jnp.bfloat16).at[targets].set(arriving, mode="drop")
    )
    audio_flag = jnp.zeros((slot_count,), jnp.int32).at[targets].set(1, mode="drop")
    text_flag = audio_flag == 0
    peer_count = lax.axis_size("seq")
    capacity = max(2, (slot_count + peer_count - 1) // peer_count)
    run_rows = table.shape[0]
    owners = token_ids // run_rows
    matches = (
        (owners[:, None] == jnp.arange(peer_count, dtype=jnp.int32)[None, :]) & text_flag[:, None]
    ).astype(jnp.int32)
    ranking = jnp.sum((jnp.cumsum(matches, axis=0) - 1) * matches, axis=1)
    bucket = jnp.where(text_flag, owners * capacity + ranking, peer_count * capacity)
    send_ids = (
        jnp.full((peer_count * capacity,), -1, jnp.int32)
        .at[bucket]
        .set(token_ids, mode="drop")
        .reshape(peer_count, capacity)
    )
    send_grad = (
        jnp.zeros((peer_count * capacity, feature_count), jnp.bfloat16)
        .at[bucket]
        .set(cotangent, mode="drop")
        .reshape(peer_count, capacity, feature_count)
    )
    first_row = lax.axis_index("seq") * run_rows
    got_ids = lax.all_to_all(send_ids, "seq", split_axis=0, concat_axis=0, tiled=True)
    got_grad = lax.all_to_all(send_grad, "seq", split_axis=0, concat_axis=0, tiled=True)
    present = got_ids >= 0
    safe_rows = jnp.where(present, got_ids - first_row, 0)
    looked = jnp.take(table, safe_rows.reshape(-1), axis=0).reshape(
        got_ids.shape + (feature_count,)
    )
    looked = jnp.where(present[..., None], looked, jnp.zeros_like(looked))
    returned = lax.all_to_all(looked, "seq", split_axis=0, concat_axis=0, tiled=True)
    returned, got_ids, got_grad = (returned, got_ids, got_grad)
    flat_rows = returned.reshape(peer_count * capacity, feature_count)
    text_rows = jnp.take(flat_rows, jnp.where(text_flag, bucket, 0), axis=0)
    llm_input = jnp.where(text_flag[:, None], text_rows, audio_part)
    present = got_ids >= 0
    local_rows = jnp.where(present, got_ids - first_row, run_rows).reshape(-1)
    gradient = (
        jnp.zeros((run_rows, feature_count), jnp.float32)
        .at[local_rows]
        .add(got_grad.reshape(-1, feature_count).astype(jnp.float32), mode="drop")
    )
    return (llm_input, gradient.astype(jnp.bfloat16))


def solution(mesh):
    return jax.shard_map(
        shards,
        mesh=mesh,
        in_specs=(
            P("seq", "vocab"),
            P(None, "vocab"),
            P("seq", "vocab"),
            P("seq", "vocab"),
            P("seq"),
            P("seq"),
            P("seq", "vocab"),
        ),
        out_specs=(P("seq", "vocab"), P("seq", "vocab")),
        check_vma=False,
    )
```

profile of v0, /device:TPU:2, one launch (start us, length us, event | category | flops | bytes accessed | tf_op | source)
XLA Modules:
  0.0 189.1 jit_solution(7601945356322872318)
XLA Ops:
  8.6 3.5 %collective-permute-start = (s32[128]{0:T(128)S(1)}, s32[128]{0:T(128)S(1)}, u32[]{:S(2)}, u32[]{:S(2)}) collective-permute-start(s32[128]{0:T(128)S(1)} %get-tuple-element.40), channel_id=1, source_target_pairs={{0,2},{2,4},{4,6},{6,8},{8,10},{10,12},{12,14},{14,16},{16,18},{18... | collective-permute-start | bytes 1544 | tf_op jit(solution)/shard_map/ppermute | solution.py:25
  12.1 0.8 fusion.52
  12.8 8.6 %collective-permute-start.2 = (bf16[15,640]{1,0:T(8,128)(2,1)S(1)}, bf16[15,640]{1,0:T(8,128)(2,1)S(1)}, u32[]{:S(2)}, u32[]{:S(2)}) collective-permute-start(bf16[15,640]{1,0:T(8,128)(2,1)S(1)} %get-tuple-element.35), channel_id=1, source_target_pairs={{2,0},{4,2},{6,4},{8,6},{10,8},{12,10},{14,12},{16,14},{18,16},{20... | collective-permute-start | bytes 57608 | tf_op jit(solution)/shard_map/ppermute | solution.py:17
  21.4 1.9 %collective-permute-start.1 = (bf16[15,640]{1,0:T(8,128)(2,1)S(1)}, bf16[15,640]{1,0:T(8,128)(2,1)S(1)}, u32[]{:S(2)}, u32[]{:S(2)}) collective-permute-start(bf16[15,640]{1,0:T(8,128)(2,1)S(1)} %get-tuple-element.36), channel_id=1, source_target_pairs={{0,2},{2,4},{4,6},{6,8},{8,10},{10,12},{12,14},{14,16},{16,18},{18... | collective-permute-start | bytes 57608 | tf_op jit(solution)/shard_map/ppermute | solution.py:16
  23.4 0.7 fusion.55
  24.9 1.4 scatter_custom_fusion
  27.2 0.7 compare_select_fusion.4
  27.9 1.6 scatter_custom_fusion.1
  29.5 0.8 all_to_all.12
  30.2 12.6 %all-to-all-start = ((s32[128,1,2]{2,1,0:T(1,128)}), s32[128,1,2]{2,1,0:T(1,128)S(1)}, u32[]{:S(2)}, u32[]{:S(2)}) async-start(s32[128,1,2]{2,1,0:T(1,128)} %bitcast.8), calls=%async_computation | async-start | bytes 131072 | tf_op jit(solution)/shard_map/all_to_all | solution.py:97
  42.9 0.7 convert_reduce_fusion.30
  43.6 2.8 %scatter_custom_fusion.3 = bf16[256,1792]{1,0:T(8,128)(2,1)S(1)} fusion(s32[256]{0:T(256)S(1)} %compare_select_fusion.4, bf16[256,1792]{1,0:T(8,128)(2,1)} %param.13, bf16[]{:T(256)} %constant.46.clone.1), kind=kCustom, calls=%fused_computation.68 | custom fusion | bytes 918016 | tf_op jit(solution)/shard_map/scatter | solution.py:93
  46.5 1.3 reshape.218
  47.7 5.9 %all-to-all-done = s32[128,1,2]{2,1,0:T(1,128)S(1)} async-done(((s32[128,1,2]{2,1,0:T(1,128)}), s32[128,1,2]{2,1,0:T(1,128)S(1)}, u32[]{:S(2)}, u32[]{:S(2)}) %all-to-all-start) | async-done | bytes 1056 | tf_op jit(solution)/shard_map/all_to_all | solution.py:97
  53.6 8.0 %all-to-all-start.2 = ((bf16[128,2,1792]{2,1,0:T(2,128)(2,1)}), bf16[128,2,1792]{2,1,0:T(2,128)(2,1)S(1)}, u32[]{:S(2)}, u32[]{:S(2)}) async-start(bf16[128,2,1792]{2,1,0:T(2,128)(2,1)} %reshape.218), calls=%async_computation.2 | async-start | bytes 1835008 | tf_op jit(solution)/shard_map/all_to_all | solution.py:98
  63.7 5.0 %gather_fusion = bf16[256,1792]{1,0:T(8,128)(2,1)S(1)} fusion(bf16[1188,1792]{1,0:T(8,128)(2,1)} %param.10, s32[1024]{0:T(1024)S(1)} %pad_clamp_fusion.1), kind=kCustom, calls=%fused_computation | custom fusion | bytes 1836032 | tf_op jit(solution)/shard_map/jit(_take)/gather | solution.py:101
  69.1 2.3 %broadcast_select_fusion.1 = bf16[128,2,1792]{2,1,0:T(2,128)(2,1)} fusion(pred[128,2]{1,0:T(8,128)(4,1)S(1)} %copy.21, bf16[128,2,1792]{2,1,0:T(2,128)(2,1)S(1)} %gather.11, pred[128,2]{1,0:T(8,128)(4,1)S(1)} %copy.23), kind=kLoop, calls=%fused_computation.25 | loop fusion | flops 917504 | bytes 1835520 | tf_op jit(solution)/shard_map/jit(_where)/select_n | solution.py:104
  71.6 18.9 %all-to-all-done.2 = bf16[128,2,1792]{2,1,0:T(2,128)(2,1)S(1)} async-done(((bf16[128,2,1792]{2,1,0:T(2,128)(2,1)}), bf16[128,2,1792]{2,1,0:T(2,128)(2,1)S(1)}, u32[]{:S(2)}, u32[]{:S(2)}) %all-to-all-start.2) | async-done | bytes 917536 | tf_op jit(solution)/shard_map/all_to_all | solution.py:98
  90.5 9.1 %all-to-all-start.1 = ((bf16[128,2,1792]{2,1,0:T(2,128)(2,1)}), bf16[128,2,1792]{2,1,0:T(2,128)(2,1)}, u32[]{:S(2)}, u32[]{:S(2)}) async-start(bf16[128,2,1792]{2,1,0:T(2,128)(2,1)} %broadcast_select_fusion.1), calls=%async_computation.1 | async-start | bytes 1835008 | tf_op jit(solution)/shard_map/all_to_all | solution.py:105
  99.9 12.9 %convert_add_fusion = f32[512,640]{1,0:T(8,128)S(1)} fusion(bf16[512,640]{1,0:T(8,128)(2,1)} %param.7, bf16[15,640]{1,0:T(8,128)(2,1)S(1)} %collective-permute-done.1, bf16[527,640]{1,0:T(8,128)(2,1)S(1)} %constant_dynamic-update-slice_fusion, f32[640]{0:T(1024)S(1)} %copy-done.30, f32[640]{0:T(1024)S(1)} %copy-done.31, f32[640]{0:T(1024)S(1)} %get-tuple-element.3, ...), kind=kLoop, calls=%fused_computation.26 | loop fusion | flops 46530560 | bytes 11895040 | tf_op jit(solution)/shard_map/add | solution.py:50
  113.3 0.8 reduce_sum.19
  114.1 2.0 %all_gather.6 = bf16[128,1280]{1,0:T(8,128)(2,1)S(1)} all-gather(bf16[128,640]{1,0:T(8,128)(2,1)S(1)} %multiply_convert_fusion), channel_id=1, replica_groups=mesh['seq'=128,'vocab'=2] {'vocab'}, dimensions={1}, use_global_device_ids=true | all-gather | bytes 491520 | tf_op jit(solution)/shard_map/all_gather | solution.py:56
  116.1 28.5 %all-gather.3.cloned.1.call-done = bf16[128,10,1792]{2,1,0:T(8,128)(2,1)} async-done(((bf16[1,10,1792]{2,1,0:T(8,128)(2,1)}), bf16[128,10,1792]{2,1,0:T(8,128)(2,1)}) %all-gather.3.cloned.1.call-update) | async-done | bytes 4587536 | tf_op jit(solution)/shard_map/all_gather | solution.py:40
  144.6 9.3 %reshape.311 = bf16[1280,1792]{1,0:T(8,128)(2,1)} reshape(bf16[128,10,1792]{2,1,0:T(8,128)(2,1)} %all-gather.3.cloned.1.call-done) | data formatting | bytes 9175040
  154.0 3.2 %convolution_convert_fusion = bf16[128,1792]{1,0:T(8,128)(2,1)S(1)} fusion(bf16[128,1280]{1,0:T(8,128)(2,1)S(1)} %all_gather.6, bf16[1280,1792]{1,0:T(8,128)(2,1)} %reshape.311), kind=kOutput, calls=%fused_computation.23 | convolution fusion | flops 587431936 | bytes 5373952 | tf_op jit(solution)/shard_map/dot_general | solution.py:38
  157.2 3.7 %collective-permute-start.3 = (bf16[128,1792]{1,0:T(8,128)(2,1)S(1)}, bf16[128,1792]{1,0:T(8,128)(2,1)}, u32[]{:S(2)}, u32[]{:S(2)}) collective-permute-start(bf16[128,1792]{1,0:T(8,128)(2,1)S(1)} %convolution_convert_fusion), channel_id=1, source_target_pairs={{0,2},{2,4},{4,6},{6,8},{8,10},{10,12},{12,14},{14,16},{16,18},{18... | collective-permute-start | bytes 1376264 | tf_op jit(solution)/shard_map/ppermute | solution.py:25
  161.5 7.2 %scatter_custom_fusion.4 = f32[1188,1792]{1,0:T(8,128)} fusion(s32[256]{0:T(256)S(1)} %bitcast.43, f32[256,1792]{1,0:T(8,128)S(1)} %reshape.303, f32[]{:T(128)} %constant.75.clone.1), kind=kCustom, calls=%fused_computation.7 | custom fusion | flops 458752 | bytes 8515588 | tf_op jit(solution)/shard_map/scatter-add | solution.py:115
  168.8 5.9 %convert_element_type.212 = bf16[1188,1792]{1,0:T(8,128)(2,1)} convert(f32[1188,1792]{1,0:T(8,128)} %scatter_custom_fusion.4) | non-fusion elementwise | flops 2128896 | bytes 12773376 | tf_op jit(solution)/shard_map/convert_element_type | solution.py:117
  174.6 2.5 %reshape.216 = bf16[256,1792]{1,0:T(8,128)(2,1)S(1)} reshape(bf16[128,2,1792]{2,1,0:T(2,128)(2,1)} %all-to-all-done.1) | data formatting | bytes 1835008 | tf_op jit(solution)/shard_map/reshape | solution.py:107
  177.1 1.3 gather_fusion.1
  178.5 2.7 %scatter_custom_fusion.2 = bf16[256,1792]{1,0:T(8,128)(2,1)S(1)} fusion(s32[256]{0:T(256)} %bitcast.42, bf16[128,1792]{1,0:T(8,128)(2,1)} %collective-permute-done.3, bf16[]{:T(256)} %constant.110, bf16[128,1792]{1,0:T(8,128)(2,1)S(1)} %convolution_convert_fusion, bf16[]{:T(256)} %constant.46.clone.1), kind=kCustom, calls=%fused_computation.44 | custom fusion | flops 1835008 | bytes 1836032 | tf_op jit(solution)/shard_map/scatter | solution.py:71
  181.2 1.1 select_select_fusion
  (127 shorter events, 6.4 us)
Async XLA Ops:
  7.2 35.7 %copy-start.3 = (bf16[31,640]{1,0:T(8,128)(2,1)S(1)}, bf16[31,640]{1,0:T(8,128)(2,1)}, u32[]{:S(2)}) copy-start(bf16[31,640]{1,0:T(8,128)(2,1)} %param.8) | copy-start | bytes 119044
  7.2 137.5 %all-gather.3.cloned.1.call-start = ((), (), s32[]{:S(2)}) async-start(), calls=%async_computation.3 | async-start | bytes 7397376 | tf_op jit(solution)/shard_map/all_gather | solution.py:40
  8.6 16.3 %collective-permute-start = (s32[128]{0:T(128)S(1)}, s32[128]{0:T(128)S(1)}, u32[]{:S(2)}, u32[]{:S(2)}) collective-permute-start(s32[128]{0:T(128)S(1)} %get-tuple-element.40), channel_id=1, source_target_pairs={{0,2},{2,4},{4,6},{6,8},{8,10},{10,12},{12,14},{14,16},{16,18},{18... | collective-permute-start | bytes 1544 | tf_op jit(solution)/shard_map/ppermute | solution.py:25
  12.8 58.8 %collective-permute-start.2 = (bf16[15,640]{1,0:T(8,128)(2,1)S(1)}, bf16[15,640]{1,0:T(8,128)(2,1)S(1)}, u32[]{:S(2)}, u32[]{:S(2)}) collective-permute-start(bf16[15,640]{1,0:T(8,128)(2,1)S(1)} %get-tuple-element.35), channel_id=1, source_target_pairs={{2,0},{4,2},{6,4},{8,6},{10,8},{12,10},{14,12},{16,14},{18,16},{20... | collective-permute-start | bytes 57608 | tf_op jit(solution)/shard_map/ppermute | solution.py:17
  21.4 78.2 %collective-permute-start.1 = (bf16[15,640]{1,0:T(8,128)(2,1)S(1)}, bf16[15,640]{1,0:T(8,128)(2,1)S(1)}, u32[]{:S(2)}, u32[]{:S(2)}) collective-permute-start(bf16[15,640]{1,0:T(8,128)(2,1)S(1)} %get-tuple-element.36), channel_id=1, source_target_pairs={{0,2},{2,4},{4,6},{6,8},{8,10},{10,12},{12,14},{14,16},{16,18},{18... | collective-permute-start | bytes 57608 | tf_op jit(solution)/shard_map/ppermute | solution.py:16
  30.2 23.4 %all-to-all-start = ((s32[128,1,2]{2,1,0:T(1,128)}), s32[128,1,2]{2,1,0:T(1,128)S(1)}, u32[]{:S(2)}, u32[]{:S(2)}) async-start(s32[128,1,2]{2,1,0:T(1,128)} %bitcast.8), calls=%async_computation | async-start | bytes 131072 | tf_op jit(solution)/shard_map/all_to_all | solution.py:97
  53.6 36.9 %all-to-all-start.2 = ((bf16[128,2,1792]{2,1,0:T(2,128)(2,1)}), bf16[128,2,1792]{2,1,0:T(2,128)(2,1)S(1)}, u32[]{:S(2)}, u32[]{:S(2)}) async-start(bf16[128,2,1792]{2,1,0:T(2,128)(2,1)} %reshape.218), calls=%async_computation.2 | async-start | bytes 1835008 | tf_op jit(solution)/shard_map/all_to_all | solution.py:98
  71.4 28.3 %copy-start.8 = (f32[640]{0:T(1024)S(1)}, f32[640]{0:T(1024)}, u32[]{:S(2)}) copy-start(f32[640]{0:T(1024)} %get-tuple-element.9) | copy-start | bytes 7684
  71.4 28.3 %copy-start.9 = (f32[640]{0:T(1024)S(1)}, f32[640]{0:T(1024)}, u32[]{:S(2)}) copy-start(f32[640]{0:T(1024)} %get-tuple-element.10) | copy-start | bytes 7684
  71.4 28.3 %copy-start.10 = (f32[640]{0:T(1024)S(1)}, f32[640]{0:T(1024)}, u32[]{:S(2)}) copy-start(f32[640]{0:T(1024)} %get-tuple-element.11) | copy-start | bytes 7684
  71.4 28.3 %copy-start.11 = (f32[640]{0:T(1024)S(1)}, f32[640]{0:T(1024)}, u32[]{:S(2)}) copy-start(f32[640]{0:T(1024)} %get-tuple-element.12) | copy-start | bytes 7684
  71.4 28.3 %copy-start.12 = (f32[640]{0:T(1024)S(1)}, f32[640]{0:T(1024)}, u32[]{:S(2)}) copy-start(f32[640]{0:T(1024)} %get-tuple-element.13) | copy-start | bytes 7684
  71.4 28.3 %copy-start.13 = (f32[640]{0:T(1024)S(1)}, f32[640]{0:T(1024)}, u32[]{:S(2)}) copy-start(f32[640]{0:T(1024)} %get-tuple-element.14) | copy-start | bytes 7684
  71.4 28.3 %copy-start.14 = (f32[640]{0:T(1024)S(1)}, f32[640]{0:T(1024)}, u32[]{:S(2)}) copy-start(f32[640]{0:T(1024)} %get-tuple-element.15) | copy-start | bytes 7684
  71.4 28.3 %copy-start.15 = (f32[640]{0:T(1024)S(1)}, f32[640]{0:T(1024)}, u32[]{:S(2)}) copy-start(f32[640]{0:T(1024)} %get-tuple-element.16) | copy-start | bytes 7684
  71.4 28.3 %copy-start.16 = (f32[640]{0:T(1024)S(1)}, f32[640]{0:T(1024)}, u32[]{:S(2)}) copy-start(f32[640]{0:T(1024)} %get-tuple-element.17) | copy-start | bytes 7684
  71.4 28.3 %copy-start.17 = (f32[640]{0:T(1024)S(1)}, f32[640]{0:T(1024)}, u32[]{:S(2)}) copy-start(f32[640]{0:T(1024)} %get-tuple-element.18) | copy-start | bytes 7684
  71.5 28.3 %copy-start.18 = (f32[640]{0:T(1024)S(1)}, f32[640]{0:T(1024)}, u32[]{:S(2)}) copy-start(f32[640]{0:T(1024)} %get-tuple-element.19) | copy-start | bytes 7684
  71.5 28.3 %copy-start.19 = (f32[640]{0:T(1024)S(1)}, f32[640]{0:T(1024)}, u32[]{:S(2)}) copy-start(f32[640]{0:T(1024)} %get-tuple-element.20) | copy-start | bytes 7684
  71.5 28.3 %copy-start.20 = (f32[640]{0:T(1024)S(1)}, f32[640]{0:T(1024)}, u32[]{:S(2)}) copy-start(f32[640]{0:T(1024)} %get-tuple-element.21) | copy-start | bytes 7684
  71.5 28.3 %copy-start.21 = (f32[640]{0:T(1024)S(1)}, f32[640]{0:T(1024)}, u32[]{:S(2)}) copy-start(f32[640]{0:T(1024)} %get-tuple-element.22) | copy-start | bytes 7684
  71.5 28.3 %copy-start.22 = (f32[640]{0:T(1024)S(1)}, f32[640]{0:T(1024)}, u32[]{:S(2)}) copy-start(f32[640]{0:T(1024)} %get-tuple-element.23) | copy-start | bytes 7684
  71.5 28.3 %copy-start.23 = (f32[640]{0:T(1024)S(1)}, f32[640]{0:T(1024)}, u32[]{:S(2)}) copy-start(f32[640]{0:T(1024)} %get-tuple-element.24) | copy-start | bytes 7684
  71.5 28.3 %copy-start.24 = (f32[640]{0:T(1024)S(1)}, f32[640]{0:T(1024)}, u32[]{:S(2)}) copy-start(f32[640]{0:T(1024)} %get-tuple-element.25) | copy-start | bytes 7684
  71.5 28.3 %copy-start.25 = (f32[640]{0:T(1024)S(1)}, f32[640]{0:T(1024)}, u32[]{:S(2)}) copy-start(f32[640]{0:T(1024)} %get-tuple-element.26) | copy-start | bytes 7684
  71.5 28.3 %copy-start.26 = (f32[640]{0:T(1024)S(1)}, f32[640]{0:T(1024)}, u32[]{:S(2)}) copy-start(f32[640]{0:T(1024)} %get-tuple-element.27) | copy-start | bytes 7684
  71.5 28.3 %copy-start.27 = (f32[640]{0:T(1024)S(1)}, f32[640]{0:T(1024)}, u32[]{:S(2)}) copy-start(f32[640]{0:T(1024)} %get-tuple-element.28) | copy-start | bytes 7684
  71.6 28.3 %copy-start.28 = (f32[640]{0:T(1024)S(1)}, f32[640]{0:T(1024)}, u32[]{:S(2)}) copy-start(f32[640]{0:T(1024)} %get-tuple-element.29) | copy-start | bytes 7684
  71.6 28.3 %copy-start.29 = (f32[640]{0:T(1024)S(1)}, f32[640]{0:T(1024)}, u32[]{:S(2)}) copy-start(f32[640]{0:T(1024)} %get-tuple-element.30) | copy-start | bytes 7684
  71.6 28.3 %copy-start.30 = (f32[640]{0:T(1024)S(1)}, f32[640]{0:T(1024)}, u32[]{:S(2)}) copy-start(f32[640]{0:T(1024)} %get-tuple-element.31) | copy-start | bytes 7684
  90.5 84.1 %all-to-all-start.1 = ((bf16[128,2,1792]{2,1,0:T(2,128)(2,1)}), bf16[128,2,1792]{2,1,0:T(2,128)(2,1)}, u32[]{:S(2)}, u32[]{:S(2)}) async-start(bf16[128,2,1792]{2,1,0:T(2,128)(2,1)} %broadcast_select_fusion.1), calls=%async_computation.1 | async-start | bytes 1835008 | tf_op jit(solution)/shard_map/all_to_all | solution.py:105
  157.2 21.3 %collective-permute-start.3 = (bf16[128,1792]{1,0:T(8,128)(2,1)S(1)}, bf16[128,1792]{1,0:T(8,128)(2,1)}, u32[]{:S(2)}, u32[]{:S(2)}) collective-permute-start(bf16[128,1792]{1,0:T(8,128)(2,1)S(1)} %convolution_convert_fusion), channel_id=1, source_target_pairs={{0,2},{2,4},{4,6},{6,8},{8,10},{10,12},{12,14},{14,16},{16,18},{18... | collective-permute-start | bytes 1376264 | tf_op jit(solution)/shard_map/ppermute | solution.py:25
  (17 other events, 257.7 us)
Sparse Core Ops, SparseCore 0:
  11.5 133.1 all-gather.2
where the time goes:
time: 191 us; the launch traced here: 189 us
  waiting for transfers between devices  54 us (28%)
  starting transfers between devices  47.6 us (25%)
  other arithmetic  38.4 us (20%)
  local copies, waits for them, and re-layouts  29.1 us (15%)
  between operations  14.9 us (8%)
  matrix products  3.17 us (2%)
  blocking collectives  2.04 us (1%)
    all_gather x1, waiting for transfers between devices, project(): lax.all_gather(proj_weight, 'seq', axis=0, tiled=True)  28.5 us
    all_to_all x1, waiting for transfers between devices, shards(): lax.all_to_all(send_grad, 'seq', split_axis=0, concat_axis=0, tiled=True)  18.9 us
    add x1, other arithmetic, shards(): activated = frames.astype(jnp.float32) + jax.nn.silu(filtered)  12.9 us
    all_to_all x1, starting transfers between devices, shards(): lax.all_to_all(send_ids, 'seq', split_axis=0, concat_axis=0, tiled=True)  12.6 us
    unnamed x84, local copies, waits for them, and re-layouts  9.57 us
    all_to_all x1, starting transfers between devices, shards(): lax.all_to_all(looked, 'seq', split_axis=0, concat_axis=0, tiled=True)  9.13 us
    ppermute x1, starting transfers between devices, extended(): after = lax.ppermute(first, axis, down)  8.61 us
    all_to_all x1, starting transfers between devices, shards(): lax.all_to_all(send_grad, 'seq', split_axis=0, concat_axis=0, tiled=True)  8.04 us
  transfers between devices with their start and end apart: 8, of which 3 were waited for; matrix products, arithmetic and copies ran while one was open for 35% of the time, Pallas kernels for 0%

commit v1 on v0

v1 whole, which is shorter than its diff:
```python
import functools

import jax
import jax.numpy as jnp
import numpy as np
from jax import lax
from jax.experimental import pallas as pl
from jax.experimental.pallas import tpu as pltpu
from jax.sharding import PartitionSpec as P

MESH = pl.DeviceIdType.MESH
BF = jnp.bfloat16
F32 = jnp.float32
NX, NZ, NY = 4, 8, 4
N_SEQ = NX * NZ * NY
PLANE = NX * NY
POOL = 4
SLOT = 256
RUN = 128
VROWS = 1188
D = 1792
NC = 2
CW = D // NC
CH = 640
FR = 512
TAPS = 31
WROWS = 10
WP = 1152
KB = NZ * WROWS


def relay_matrix():
    m = np.zeros((SLOT, SLOT), np.float32)
    for z in range(NZ):
        for k in range(2):
            for p in range(PLANE):
                m[p * 16 + k * 8 + z, z * 32 + k * 16 + p] = 1
    return m


def channel_matrix():
    m = np.zeros((CH, CH), np.float32)
    for c in range(CH):
        x, z, y, i = c // 320, (c % 320) // 40, (c % 40) // 10, c % 10
        inner = z * 8 + i if i < 8 else 64 + z * 2 + i - 8
        m[c, (x * 4 + y) * KB + inner] = 1
    return m


def pack_matrices():
    m = np.zeros((9, 16, 16), np.float32)
    for i in range(8):
        m[0, i, i] = 1
        m[1, 8 + i, i] = 1
    for g in range(7):
        for i in range(2):
            m[2 + g, 2 * g + i, 8 + i] = 1
    return m.reshape(9 * 16, 16)


def unpack_matrices():
    top = np.zeros((2, 64, 128), np.float32)
    low = np.zeros((7, 16, 128), np.float32)
    for z in range(NZ):
        for i in range(8):
            top[0, z * 8 + i, z * 16 + i] = 1
            top[1, z * 8 + i, z * 16 + 8 + i] = 1
        for g in range(7):
            for i in range(2):
                low[g, z * 2 + i, z * 16 + 2 * g + i] = 1
    return np.concatenate([top.reshape(128, 128), low.reshape(112, 128)])


def mm(a, b):
    return jnp.dot(a, b, preferred_element_type=F32)


def comm_kernel(
    ids_ref, pos_ref, frames_ref, cw_ref, w_ref, relay_ref, back_ref, chan_ref, pack_ref, unpack_ref,
    cot_hbm, table_hbm,
    llm_hbm, got_hbm, row_ref,
    cot, table, sel_s, snd1, rcv1, snd2, rcv2, bsnd1, brcv1, bsnd2, brcv2,
    idsnd, idrcv, idcomp, idall, stsnd, strcv, halo, ext, cwf, act, pooled, plo, plp,
    wpadf, wpk, wrz, wst, wfull, xs, llm,
    loc_sem, st_sem, halo_sem, idz_s, idz_r, idp_s, idp_r, wz_s, wz_r,
    fz_s, fz_r, fp_s, fp_r, bp_s, bp_r, bz_s, bz_r,
    w1_s, w1_r, w1x_s, w1x_r, w2_s, w2_r, w2x_s, w2x_r, pool_s, pool_r,
):
    s = lax.axis_index("seq")
    v = lax.axis_index("vocab")
    x, z, y = s // 32, (s // 4) % 8, s % 4
    p = x * 4 + y

    def at(xx, zz, yy):
        return ((xx * 8 + zz) * 4 + yy, v)

    def zpeer(d):
        return at(x, lax.rem(z + d, 8), y)

    def ppeer(j):
        return at(lax.rem(x + j // 4, 4), z, lax.rem(y + lax.rem(j, 4), 4))

    def pplace(j):
        return lax.rem(x + j // 4, 4) * 4 + lax.rem(y + lax.rem(j, 4), 4)

    nxt = (lax.rem(s + 1, N_SEQ), v)
    prv = (lax.rem(s + N_SEQ - 1, N_SEQ), v)
    other = (s, 1 - v)

    def remote(src, dst, ss, rs, dev):
        return pltpu.make_async_remote_copy(
            src_ref=src, dst_ref=dst, send_sem=ss, recv_sem=rs, device_id=dev, device_id_type=MESH
        )

    bar = pltpu.get_barrier_semaphore()
    for d in range(1, 8):
        pl.semaphore_signal(bar, inc=1, device_id=zpeer(d), device_id_type=MESH)

    def greet(j, c):
        pl.semaphore_signal(bar, inc=1, device_id=ppeer(j), device_id_type=MESH)
        return c

    lax.fori_loop(1, PLANE, greet, 0)
    for dev in (nxt, prv, other):
        pl.semaphore_signal(bar, inc=1, device_id=dev, device_id_type=MESH)

    cot_cp = pltpu.make_async_copy(cot_hbm, cot, loc_sem.at[0])
    cot_cp.start()
    table_cp = pltpu.make_async_copy(table_hbm, table, loc_sem.at[1])
    table_cp.start()

    bcol = lax.broadcasted_iota(jnp.int32, (SLOT, 1), 0)
    bz, bk, bp = bcol >> 5, (bcol >> 4) & 1, bcol & 15
    low = (((bp >> 2) * 8 + bz) * 4 + (bp & 3)) * VROWS
    rel = ids_ref[...] - low
    qi = lax.broadcasted_iota(jnp.int32, (SLOT, SLOT), 1).astype(F32)
    hit = (rel >= 0) & (rel < VROWS)
    first = jnp.min(jnp.where(hit, qi, 4096.0), axis=1, keepdims=True)
    last = jnp.max(jnp.where(hit, qi, -1.0), axis=1, keepdims=True)
    chosen = jnp.where(bk == 0, first, jnp.where(last > first, last, -1.0))
    picked = qi == chosen
    sel_s[...] = jnp.where(picked, 1.0, 0.0).astype(BF)
    relf = jnp.where(picked, (rel + 1).astype(F32), 0.0)

    wpadf[...] = jnp.zeros_like(wpadf)
    wpadf[0:WROWS, :] = w_ref[...].astype(F32)
    wp = wpadf[...].astype(BF)
    half = D // 2
    wpk[:, 0:half] = (mm(pack_ref[0:16], wp[:, 0:half]) + mm(pack_ref[16:32], wp[:, half:])).astype(BF)
    tail = jnp.zeros((16, 256), F32)
    for g in range(7):
        tail = tail + mm(pack_ref[32 + 16 * g : 48 + 16 * g], wp[:, 256 * g : 256 * g + 256])
    wpk[:, half:] = tail.astype(BF)
    zrow16 = pl.multiple_of(z * 16, 16)
    wrz[pl.ds(zrow16, 16), :] = wpk[...]

    start = pos_ref[0:1, 0:1]
    stsnd[...] = jnp.broadcast_to(start, (8, 128))

    pl.semaphore_wait(bar, 7 + PLANE - 1 + 3)

    st_cp = remote(stsnd, strcv, st_sem.at[0], st_sem.at[1], nxt)
    st_cp.start()
    up_cp = remote(frames_ref.at[pl.ds(FR - 16, 16)], halo.at[0], halo_sem.at[0], halo_sem.at[1], nxt)
    dn_cp = remote(frames_ref.at[pl.ds(0, 16)], halo.at[1], halo_sem.at[2], halo_sem.at[3], prv)
    up_cp.start()
    dn_cp.start()
    wz_cps = [
        remote(wpk, wrz.at[pl.ds(zrow16, 16)], wz_s.at[d], wz_r.at[d], zpeer(d)) for d in range(1, 8)
    ]
    for cp in wz_cps:
        cp.start()

    zrow = pl.multiple_of(z * 32, 32)
    cot_cp.wait()
    fz_cps = []
    for c in range(NC):
        snd1[c] = mm(sel_s[...], cot[:, c * CW : (c + 1) * CW]).astype(BF)

    st_cp.wait()
    before = jnp.where(s > 0, strcv[0:1, 0:1], -4096)
    slot = s * SLOT + lax.broadcasted_iota(jnp.int32, (1, SLOT), 1)
    audio = ((slot >= start) & (slot < start + RUN)) | ((slot >= before) & (slot < before + RUN))
    idv = jnp.sum(jnp.where(audio, 0.0, relf), axis=1, keepdims=True) - 1.0
    brow = lax.broadcasted_iota(jnp.int32, (SLOT, SLOT), 0)
    qcol = lax.broadcasted_iota(jnp.int32, (SLOT, SLOT), 1)
    diag = brow == qcol
    idrow = jnp.sum(jnp.where(diag, idv, 0.0), axis=0, keepdims=True)
    eight = lax.broadcasted_iota(jnp.int32, (8, 128), 0)
    idsnd[...] = jnp.where(eight == 0, idrow[:, 0:128], idrow[:, 128:256]).astype(jnp.int32)
    zrow8 = pl.multiple_of(z * 8, 8)
    idrcv[pl.ds(zrow8, 8), :] = idsnd[...]
    idz_cps = [
        remote(idsnd, idrcv.at[pl.ds(zrow8, 8)], idz_s.at[d], idz_r.at[d], zpeer(d)) for d in range(1, 8)
    ]
    for cp in idz_cps:
        cp.start()

    for c in range(NC):
        for d in (1, 7, 2, 6, 3, 5, 4):
            to = pl.multiple_of(lax.rem(z + d, 8) * 32, 32)
            cp = remote(
                snd1.at[c, pl.ds(to, 32)], rcv1.at[c, pl.ds(zrow, 32)], fz_s.at[c, d], fz_r.at[c, d], zpeer(d)
            )
            cp.start()
            fz_cps.append(cp)
        rcv1[c, pl.ds(zrow, 32), :] = snd1[c, pl.ds(zrow, 32), :]

    for cp in idz_cps:
        cp.wait()
    even = idrcv[pl.ds(0, 8, stride=8), :]
    odd = idrcv[pl.ds(1, 8, stride=8), :]
    idcomp[...] = jnp.where(z < 4, even, odd)
    prow8 = pl.multiple_of(p * 8, 8)
    idall[pl.ds(prow8, 8), :] = idcomp[...]

    def idp_copy(j):
        return remote(idcomp, idall.at[pl.ds(prow8, 8)], idp_s.at[j], idp_r.at[j], ppeer(j))

    def plane(fn):
        def body(j, c):
            fn(j)
            return c

        lax.fori_loop(1, PLANE, body, 0)

    plane(lambda j: idp_copy(j).start())

    for cp in wz_cps:
        cp.wait()
    prow80 = pl.multiple_of(p * KB, 16)
    packed = wrz[...]
    for c in range(NC):
        wst[c, 0:64, :] = mm(unpack_ref[64 * c : 64 * c + 64], packed[:, 0:half]).astype(BF)
    for g in range(7):
        piece = mm(unpack_ref[128 + 16 * g : 144 + 16 * g], packed[:, half:]).astype(BF)
        for b in range(2):
            col = 256 * g + 128 * b
            c, off = col // CW, col % CW
            wst[c, 64:KB, off : off + 128] = piece[:, 128 * b : 128 * b + 128]

    for c in range(NC):
        wfull[c, pl.ds(prow80, KB), :] = wst[c]

    def wplace(c, f, g):
        ff, gg = lax.rem((x if c == 0 else y) + f, 4), lax.rem((y if c == 0 else x) + g, 4)
        return ff * 4 + gg if c == 0 else gg * 4 + ff

    def wpeer(c, f, g):
        ff, gg = lax.rem((x if c == 0 else y) + f, 4), lax.rem((y if c == 0 else x) + g, 4)
        return at(ff, z, gg) if c == 0 else at(gg, z, ff)

    def wblock(c, f, g, lo=0, n=KB):
        return wfull.at[c, pl.ds(pl.multiple_of(wplace(c, f, g) * KB + lo, 16), n)]

    def wsend(c, block, sems, dev):
        cp = remote(block, block, sems[0], sems[1], dev)
        cp.start()
        return cp

    wsends = []

    for c in range(NC):
        for i, f in enumerate((1, 3)):
            wsends.append(wsend(c, wblock(c, 0, 0), (w1_s.at[c, i], w1_r.at[c, i]), wpeer(c, f, 0)))
    for c in range(NC):
        for i, g in enumerate((1, 3)):
            wsends.append(wsend(c, wblock(c, 0, 0), (w2_s.at[c, i, 0], w2_r.at[c, i, 0]), wpeer(c, 0, g)))

    def wgot(block, sem):
        remote(block, block, w1_s.at[0, 0], sem, other).wait_recv()

    plane(lambda j: idp_copy(j).wait())
    dup = []
    for i in range(PLANE):
        piece = idall[8 * i : 8 * i + 8, :]
        dup += [piece, piece]
    every = jnp.concatenate(dup, axis=0)
    lane = lax.broadcasted_iota(jnp.int32, (SLOT, 128), 1)
    rrow = lax.broadcasted_iota(jnp.int32, (SLOT, 128), 0)
    want = lax.rem(z, 4) * 32 + ((rrow >> 3) & 1) * 16 + p
    rowid = jnp.sum(jnp.where(lane == want, every, 0).astype(F32), axis=1, keepdims=True)
    row_ref[...] = jnp.broadcast_to(
        jnp.sum(jnp.where(diag, rowid, 0.0), axis=0, keepdims=True).astype(jnp.int32), (8, SLOT)
    )
    vi = lax.broadcasted_iota(jnp.int32, (SLOT, VROWS), 1)
    look = jnp.where(vi == rowid.astype(jnp.int32), 1.0, 0.0).astype(BF)
    table_cp.wait()
    prow16 = pl.multiple_of(p * 16, 16)

    def bp_copy(c, j):
        to = pl.multiple_of(pplace(j) * 16, 16)
        return remote(
            bsnd1.at[c, pl.ds(to, 16)], brcv1.at[c, pl.ds(prow16, 16)], bp_s.at[c, j], bp_r.at[c, j], ppeer(j)
        )

    for c in range(NC):
        bsnd1[c] = mm(look, table[:, c * CW : (c + 1) * CW]).astype(BF)
        plane(lambda j: bp_copy(c, j).start())
        brcv1[c, pl.ds(prow16, 16), :] = bsnd1[c, pl.ds(prow16, 16), :]

    for c in range(NC):
        wgot(wblock(c, 3, 0), w1_r.at[c, 0])
        wsends.append(wsend(c, wblock(c, 3, 0, 0, 48), (w1x_s.at[c, 0], w1x_r.at[c, 0]), wpeer(c, 1, 0)))
        wgot(wblock(c, 1, 0), w1_r.at[c, 1])
        wsends.append(wsend(c, wblock(c, 1, 0, 48, 32), (w1x_s.at[c, 1], w1x_r.at[c, 1]), wpeer(c, 3, 0)))
        for f in (1, 3):
            for i, g in enumerate((1, 3)):
                wsends.append(wsend(c, wblock(c, f, 0), (w2_s.at[c, i, f], w2_r.at[c, i, f]), wpeer(c, 0, g)))

    up_cp.wait()
    dn_cp.wait()
    for l in range(5):
        cols = slice(128 * l, 128 * l + 128)
        ext[l, 16 : 16 + FR, :] = frames_ref[:, cols].astype(F32)
        ext[l, 0:16, :] = jnp.where(s > 0, halo[0, :, cols].astype(F32), 0.0)
        ext[l, 16 + FR : 32 + FR, :] = jnp.where(s < N_SEQ - 1, halo[1, :, cols].astype(F32), 0.0)
        cwf[l, 0:TAPS, :] = cw_ref[:, cols].astype(F32)

    def conv(i, carry):
        l, rb = i // 8, lax.rem(i, 8)
        r0 = pl.multiple_of(rb * 64, 64)
        acc = jnp.zeros((64, 128), F32)
        for j in range(TAPS):
            acc = acc + ext[l, pl.ds(r0 + (j + 1), 64), :] * cwf[l, pl.ds(j, 1), :]
        act[...] = ext[l, pl.ds(r0 + 16, 64), :] + acc / (1.0 + jnp.exp(-acc))
        total = act[pl.ds(0, 16, stride=4), :]
        for k in range(1, POOL):
            total = total + act[pl.ds(k, 16, stride=4), :]
        pooled[pl.ds(pl.multiple_of(rb * 16, 16), 16), pl.ds(pl.multiple_of(l * 128, 128), 128)] = (
            total * (1.0 / POOL)
        ).astype(BF)
        return carry

    lax.fori_loop(0, 40, conv, 0)
    plo[v] = mm(pooled[...], chan_ref[...]).astype(BF)
    core_cp = remote(plo.at[v], plo.at[v], pool_s.at[0], pool_r.at[0], other)
    next_cp = remote(plo.at[v], plp.at[v], pool_s.at[1], pool_r.at[1], nxt)
    core_cp.start()
    next_cp.start()

    def fp_copy(c, j):
        to = pl.multiple_of(pplace(j) * 16, 16)
        return remote(
            snd2.at[c, pl.ds(to, 16)], rcv2.at[c, pl.ds(prow16, 16)], fp_s.at[c, j], fp_r.at[c, j], ppeer(j)
        )

    def forward(c):
        for cp in fz_cps[7 * c : 7 * c + 7]:
            cp.wait()
        snd2[c] = mm(relay_ref[...], rcv1[c]).astype(BF)
        plane(lambda j: fp_copy(c, j).start())
        rcv2[c, pl.ds(prow16, 16), :] = snd2[c, pl.ds(prow16, 16), :]

    bz_cps = []

    def back(c):
        plane(lambda j: bp_copy(c, j).wait())
        bsnd2[c] = mm(back_ref[...], brcv1[c]).astype(BF)
        for d in (1, 7, 2, 6, 3, 5, 4):
            to = pl.multiple_of(lax.rem(z + d, 8) * 32, 32)
            cp = remote(
                bsnd2.at[c, pl.ds(to, 32)], brcv2.at[c, pl.ds(zrow, 32)], bz_s.at[c, d], bz_r.at[c, d], zpeer(d)
            )
            cp.start()
            bz_cps.append(cp)
        brcv2[c, pl.ds(zrow, 32), :] = bsnd2[c, pl.ds(zrow, 32), :]

    back(0)
    back(1)

    for c in range(NC):
        wgot(wblock(c, 2, 0, 0, 48), w1x_r.at[c, 0])
        wgot(wblock(c, 2, 0, 48, 32), w1x_r.at[c, 1])
        for i, g in enumerate((1, 3)):
            wsends.append(wsend(c, wblock(c, 2, 0), (w2_s.at[c, i, 2], w2_r.at[c, i, 2]), wpeer(c, 0, g)))

    def w2relay(c, f):
        i, near, to = (0, 3, 1) if f < 2 else (1, 1, 3)
        wgot(wblock(c, f, near), w2_r.at[c, i, f])
        wsends.append(wsend(c, wblock(c, f, near), (w2x_s.at[c, f], w2x_r.at[c, f]), wpeer(c, 0, to)))

    for c in range(NC):
        w2relay(c, 0)

    forward(0)

    for f in (1, 3, 2):
        for c in range(NC):
            w2relay(c, f)

    forward(1)

    next_cp.wait()
    fwd_cp = remote(plp.at[v], plp.at[v], pool_s.at[2], pool_r.at[2], other)
    fwd_cp.start()
    core_cp.wait()
    fwd_cp.wait()
    qslot = s * SLOT + lax.broadcasted_iota(jnp.int32, (SLOT, RUN), 0)
    prun = lax.broadcasted_iota(jnp.int32, (SLOT, RUN), 1)
    own_sel = jnp.where(qslot == start + prun, 1.0, 0.0).astype(BF)
    prev_sel = jnp.where(qslot == before + prun, 1.0, 0.0).astype(BF)
    for h in range(2):
        xs[:, h * CH : (h + 1) * CH] = (mm(own_sel, plo[h]) + mm(prev_sel, plp[h])).astype(BF)

    for c in range(NC):
        for f in range(4):
            i, near = (1, 1) if f < 2 else (0, 3)
            wgot(wblock(c, f, near), w2_r.at[c, i, f])
            wgot(wblock(c, f, 2), w2x_r.at[c, f])
        llm[c] = mm(xs[...], wfull[c]).astype(BF)

    outs = []
    for c in range(NC):
        plane(lambda j: fp_copy(c, j).wait())
        cp = pltpu.make_async_copy(rcv2.at[c], got_hbm.at[:, pl.ds(c * CW, CW)], loc_sem.at[2 + c])
        cp.start()
        outs.append(cp)
    for c in range(NC):
        for cp in bz_cps[7 * c : 7 * c + 7]:
            cp.wait()
        text = lax.dot_general(sel_s[...], brcv2[c], (((0,), (0,)), ((), ())), preferred_element_type=F32)
        llm[c] = (text + llm[c].astype(F32)).astype(BF)
        cp = pltpu.make_async_copy(llm.at[c], llm_hbm.at[:, pl.ds(c * CW, CW)], loc_sem.at[4 + c])
        cp.start()
        outs.append(cp)
    for cp in wsends:
        cp.wait_send()
    for cp in outs:
        cp.wait()


def out_kernel(row_ref, got_ref, llm_ref, out_ref, grad_ref, place):
    @pl.when(pl.program_id(0) == 0)
    def _():
        vi = lax.broadcasted_iota(jnp.int32, (VROWS, SLOT), 0)
        place[...] = jnp.where(vi == row_ref[0:1, :], 1.0, 0.0).astype(BF)

    grad_ref[...] = mm(place[...], got_ref[...]).astype(BF)
    out_ref[...] = llm_ref[...]


def shards(frames, conv_weight, proj_weight, table, audio_pos, token_ids, cotangent):
    relay = relay_matrix()
    consts = [relay, relay.T, channel_matrix(), pack_matrices(), unpack_matrices()]
    consts = [jnp.asarray(m, dtype=BF) for m in consts]
    vm = pl.BlockSpec(memory_space=pltpu.VMEM)
    hbm = pl.BlockSpec(memory_space=pl.ANY)
    dma = pltpu.SemaphoreType.DMA
    wide = pltpu.VMEM((NC, SLOT, CW), BF)
    llm, got, rows = pl.pallas_call(
        comm_kernel,
        out_shape=[
            jax.ShapeDtypeStruct((SLOT, D), BF),
            jax.ShapeDtypeStruct((SLOT, D), BF),
            jax.ShapeDtypeStruct((8, SLOT), jnp.int32),
        ],
        in_specs=[vm] * 10 + [hbm] * 2,
        out_specs=[hbm, hbm, vm],
        scratch_shapes=[
            pltpu.VMEM((SLOT, D), BF),
            pltpu.VMEM((VROWS, D), BF),
            pltpu.VMEM((SLOT, SLOT), BF),
            wide, wide, wide, wide, wide, wide, wide, wide,
            pltpu.VMEM((8, 128), jnp.int32),
            pltpu.VMEM((64, 128), jnp.int32),
            pltpu.VMEM((8, 128), jnp.int32),
            pltpu.VMEM((128, 128), jnp.int32),
            pltpu.VMEM((8, 128), jnp.int32),
            pltpu.VMEM((8, 128), jnp.int32),
            pltpu.VMEM((2, 16, CH), BF),
            pltpu.VMEM((5, FR + 32, 128), F32),
            pltpu.VMEM((5, 32, 128), F32),
            pltpu.VMEM((64, 128), F32),
            pltpu.VMEM((RUN, CH), BF),
            pltpu.VMEM((2, RUN, CH), BF),
            pltpu.VMEM((2, RUN, CH), BF),
            pltpu.VMEM((16, D), F32),
            pltpu.VMEM((16, WP), BF),
            pltpu.VMEM((128, WP), BF),
            pltpu.VMEM((NC, KB, CW), BF),
            pltpu.VMEM((NC, PLANE * KB, CW), BF),
            pltpu.VMEM((SLOT, 2 * CH), BF),
            wide,
            dma((6,)), dma((2,)), dma((4,)),
            dma((8,)), dma((8,)), dma((16,)), dma((16,)), dma((8,)), dma((8,)),
            dma((2, 8)), dma((2, 8)), dma((2, 16)), dma((2, 16)),
            dma((2, 16)), dma((2, 16)), dma((2, 8)), dma((2, 8)),
            dma((2, 2)), dma((2, 2)), dma((2, 2)), dma((2, 2)),
            dma((2, 2, 4)), dma((2, 2, 4)), dma((2, 4)), dma((2, 4)),
            dma((3,)), dma((3,)),
        ],
        compiler_params=pltpu.CompilerParams(
            collective_id=0, has_side_effects=True, vmem_limit_bytes=48 * 1024 * 1024
        ),
        name="exchange",
    )(
        token_ids.reshape(1, SLOT), audio_pos.reshape(1, RUN), frames, conv_weight, proj_weight, *consts,
        cotangent, table,
    )
    tile = 256
    return pl.pallas_call(
        out_kernel,
        grid=(D // tile,),
        out_shape=[jax.ShapeDtypeStruct((SLOT, D), BF), jax.ShapeDtypeStruct((VROWS, D), BF)],
        in_specs=[
            pl.BlockSpec((8, SLOT), lambda i: (0, 0)),
            pl.BlockSpec((SLOT, tile), lambda i: (0, i)),
            pl.BlockSpec((SLOT, tile), lambda i: (0, i)),
        ],
        out_specs=[
            pl.BlockSpec((SLOT, tile), lambda i: (0, i)),
            pl.BlockSpec((VROWS, tile), lambda i: (0, i)),
        ],
        scratch_shapes=[pltpu.VMEM((VROWS, SLOT), BF)],
        compiler_params=pltpu.CompilerParams(vmem_limit_bytes=24 * 1024 * 1024),
        name="write",
    )(rows, got, llm)


def solution(mesh):
    return jax.shard_map(
        shards,
        mesh=mesh,
        in_specs=(
            P("seq", "vocab"),
            P(None, "vocab"),
            P("seq", "vocab"),
            P("seq", "vocab"),
            P("seq"),
            P("seq"),
            P("seq", "vocab"),
        ),
        out_specs=(P("seq", "vocab"), P("seq", "vocab")),
        check_vma=False,
    )
```

time: 191 us -> 89.3 us (0.47)
  Pallas kernels: 0 us -> 78.3 us
  waiting for transfers between devices: 54 us -> 0 us
  starting transfers between devices: 47.6 us -> 0 us
  other arithmetic: 38.4 us -> 0 us
  local copies, waits for them, and re-layouts: 29.1 us -> 9.74 us
  between operations: 14.9 us -> 0.66 us
  matrix products: 3.17 us -> 0 us
  blocking collectives: 2.04 us -> 0 us
    pallas_call x0 -> x2, Pallas kernels: none -> 78.3 us  [the longest x1 73.5 us: shards(): pl.pallas_call(comm_kernel, out_shape=[jax.ShapeDtypeStruct((SLOT, D), BF...]
    all_to_all x3 -> x0, starting transfers between devices: 29.8 us -> none  [the longest x1 12.6 us: shards(): lax.all_to_all(send_ids, 'seq', split_axis=0, concat_axis=0, tiled=True)]
    all_gather x1 -> x0, waiting for transfers between devices: 28.5 us -> none  [project(): lax.all_gather(proj_weight, 'seq', axis=0, tiled=True)]
    all_to_all x3 -> x0, waiting for transfers between devices: 24.8 us -> none  [the longest x1 18.9 us: shards(): lax.all_to_all(send_grad, 'seq', split_axis=0, concat_axis=0, tiled=True)]
    ppermute x4 -> x0, starting transfers between devices: 17.7 us -> none  [the longest x1 8.61 us: extended(): after = lax.ppermute(first, axis, down)]
    add x1 -> x0, other arithmetic: 12.9 us -> none  [shards(): activated = frames.astype(jnp.float32) + jax.nn.silu(filtered)]
    scatter-add x1 -> x0, other arithmetic: 7.21 us -> none  [shards(): gradient = jnp.zeros((run_rows, feature_count), jnp.float32).at[local_row...]
    gather x3 -> x0, local copies, waits for them, and re-layouts: 6.69 us -> none  [the longest x2 5.36 us: shards(): jnp.take(table, safe_rows.reshape(-1), axis=0)]
  transfers between devices with their start and end apart: 8 -> 0, of which waited for: 3 -> 0; matrix products, arithmetic and copies ran while one was open for 35% -> 0% of each run, Pallas kernels for 0% -> 0%
where the time goes in v1:
time: 89.3 us; the launch traced here: 88.7 us
  Pallas kernels  78.3 us (88%)
  local copies, waits for them, and re-layouts  9.74 us (11%)
    pallas_call x1, Pallas kernels, shards(): pl.pallas_call(comm_kernel, out_shape=[jax.ShapeDtypeStruct((SLOT, D), BF...  73.5 us
    unnamed x22, local copies, waits for them, and re-layouts  9.74 us
    pallas_call x1, Pallas kernels, shards(): pl.pallas_call(out_kernel, grid=(D // tile,), out_shape=[jax.ShapeDtypeSt...  4.82 us

profile of v1, /device:TPU:2, one launch (start us, length us, event | category | flops | bytes accessed | tf_op | source)
XLA Modules:
  0.0 88.7 jit_solution(1828852228369700232)
XLA Ops:
  0.6 0.0 copy-start
  0.6 1.2 %copy-done = bf16[256,1792]{1,0:T(8,128)(2,1)S(1)} copy-done((bf16[256,1792]{1,0:T(8,128)(2,1)S(1)}, bf16[256,1792]{1,0:T(8,128)(2,1)}, u32[]{:S(2)}) %copy-start) | copy-done | bytes 917528
  1.8 0.0 copy-start.1
  1.8 1.1 %copy-done.1 = bf16[640,640]{1,0:T(8,128)(2,1)S(1)} copy-done((bf16[640,640]{1,0:T(8,128)(2,1)S(1)}, bf16[640,640]{1,0:T(8,128)(2,1)}, u32[]{:S(2)}) %copy-start.1) | copy-done | bytes 819224
  3.0 0.0 copy-start.2
  3.0 1.1 %copy-done.2 = bf16[512,640]{1,0:T(8,128)(2,1)S(1)} copy-done((bf16[512,640]{1,0:T(8,128)(2,1)S(1)}, bf16[512,640]{1,0:T(8,128)(2,1)}, u32[]{:S(2)}) %copy-start.2) | copy-done | bytes 655384
  4.0 0.0 copy-start.3
  4.0 0.9 %copy-done.3 = bf16[256,256]{1,0:T(8,128)(2,1)S(1)} copy-done((bf16[256,256]{1,0:T(8,128)(2,1)S(1)}, bf16[256,256]{1,0:T(8,128)(2,1)}, u32[]{:S(2)}) %copy-start.3) | copy-done | bytes 131096
  5.0 0.0 copy-start.4
  5.0 0.9 %copy-done.4 = bf16[256,256]{1,0:T(8,128)(2,1)S(1)} copy-done((bf16[256,256]{1,0:T(8,128)(2,1)S(1)}, bf16[256,256]{1,0:T(8,128)(2,1)}, u32[]{:S(2)}) %copy-start.4) | copy-done | bytes 131096
  5.9 0.0 copy-start.5
  5.9 0.8 copy-done.5
  6.7 0.0 copy-start.6
  6.7 0.8 copy-done.6
  7.5 0.0 copy-start.7
  7.5 0.8 copy-done.7
  8.3 0.0 copy-start.8
  8.3 0.8 copy-done.8
  9.1 0.0 copy-start.9
  9.1 0.7 copy-done.9
  9.7 0.0 copy-start.10
  9.7 0.7 copy-done.10
  10.4 73.5 %exchange.1 = (bf16[256,1792]{1,0:T(8,128)(2,1)S(1)}, bf16[256,1792]{1,0:T(8,128)(2,1)S(1)}, s32[8,256]{1,0:T(8,128)S(1)}) custom-call(s32[1,256]{1,0:T(1,128)S(1)} %bitcast.2, s32[1,128]{1,0:T(1,128)S(1)} %bitcast.3, bf16[512,640]{1,0:T(8,128)(2,1)S(1)} %copy-done.2, bf16[31,640]{1,0:T(8,128)(2,1)S(1)} %copy-done.7, bf16[10,1792]{1,0:T(8,128)(2,1)S(1)} %copy-done.6, ...), custom_call_target="tpu_custom_call" | custom-call | tf_op jit(solution)/shard_map/exchange/pallas_call | solution.py:451
  83.9 4.8 %write.1 = (bf16[256,1792]{1,0:T(8,128)(2,1)}, bf16[1188,1792]{1,0:T(8,128)(2,1)}) custom-call(s32[8,256]{1,0:T(8,128)S(1)} %get-tuple-element.5.row_ref, bf16[256,1792]{1,0:T(8,128)(2,1)S(1)} %get-tuple-element.6.got_ref, bf16[256,1792]{1,0:T(8,128)(2,1)S(1)} %get-tuple-element.7.llm_ref), custom_call_target="tpu_custom_call" | custom-call | tf_op jit(solution)/shard_map/write/pallas_call | solution.py:502
Async XLA Ops:
  0.6 1.2 %copy-start = (bf16[256,1792]{1,0:T(8,128)(2,1)S(1)}, bf16[256,1792]{1,0:T(8,128)(2,1)}, u32[]{:S(2)}) copy-start(bf16[256,1792]{1,0:T(8,128)(2,1)} %cot_hbm.1) | copy-start | bytes 2752516
  1.8 1.1 %copy-start.1 = (bf16[640,640]{1,0:T(8,128)(2,1)S(1)}, bf16[640,640]{1,0:T(8,128)(2,1)}, u32[]{:S(2)}) copy-start(bf16[640,640]{1,0:T(8,128)(2,1)} %constant.12.clone.chan_ref) | copy-start | bytes 2457604
  3.0 1.1 %copy-start.2 = (bf16[512,640]{1,0:T(8,128)(2,1)S(1)}, bf16[512,640]{1,0:T(8,128)(2,1)}, u32[]{:S(2)}) copy-start(bf16[512,640]{1,0:T(8,128)(2,1)} %frames_ref.1) | copy-start | bytes 1966084
  4.0 0.9 %copy-start.3 = (bf16[256,256]{1,0:T(8,128)(2,1)S(1)}, bf16[256,256]{1,0:T(8,128)(2,1)}, u32[]{:S(2)}) copy-start(bf16[256,256]{1,0:T(8,128)(2,1)} %constant.11.clone.back_ref) | copy-start | bytes 393220
  5.0 0.9 %copy-start.4 = (bf16[256,256]{1,0:T(8,128)(2,1)S(1)}, bf16[256,256]{1,0:T(8,128)(2,1)}, u32[]{:S(2)}) copy-start(bf16[256,256]{1,0:T(8,128)(2,1)} %constant.10.clone.relay_ref) | copy-start | bytes 393220
  5.9 0.8 copy-start.5
  6.7 0.8 copy-start.6
  7.5 0.8 copy-start.7
  8.3 0.8 copy-start.8
  9.1 0.7 copy-start.9
  9.7 0.7 copy-start.10

commit v2 on v0

v2 whole, which is shorter than its diff:
```python
import functools

import jax
import jax.numpy as jnp
import numpy as np
from jax import lax
from jax.experimental import pallas as pl
from jax.experimental.pallas import tpu as pltpu
from jax.sharding import PartitionSpec as P

MESH = pl.DeviceIdType.MESH
BF = jnp.bfloat16
F32 = jnp.float32
NX, NZ, NY = 4, 8, 4
N_SEQ = NX * NZ * NY
PLANE = NX * NY
POOL = 4
SLOT = 256
RUN = 128
VROWS = 1188
D = 1792
NC = 2
CW = D // NC
CH = 640
FR = 512
TAPS = 31
WROWS = 10
WP = 1152
KB = NZ * WROWS
TILE = 256
VMEM_LIMIT = 60 * 1024 * 1024


def relay_matrix():
    m = np.zeros((SLOT, SLOT), np.float32)
    for z in range(NZ):
        for k in range(2):
            for p in range(PLANE):
                m[p * 16 + k * 8 + z, z * 32 + k * 16 + p] = 1
    return m


def channel_matrix():
    m = np.zeros((CH, CH), np.float32)
    for c in range(CH):
        x, z, y, i = c // 320, (c % 320) // 40, (c % 40) // 10, c % 10
        inner = z * 8 + i if i < 8 else 64 + z * 2 + i - 8
        m[c, (x * 4 + y) * KB + inner] = 1
    return m


def pack_matrices():
    m = np.zeros((9, 16, 16), np.float32)
    for i in range(8):
        m[0, i, i] = 1
        m[1, 8 + i, i] = 1
    for g in range(7):
        for i in range(2):
            m[2 + g, 2 * g + i, 8 + i] = 1
    return m.reshape(9 * 16, 16)


def unpack_matrices():
    top = np.zeros((2, 64, 128), np.float32)
    low = np.zeros((7, 16, 128), np.float32)
    for z in range(NZ):
        for i in range(8):
            top[0, z * 8 + i, z * 16 + i] = 1
            top[1, z * 8 + i, z * 16 + 8 + i] = 1
        for g in range(7):
            for i in range(2):
                low[g, z * 2 + i, z * 16 + 2 * g + i] = 1
    return np.concatenate([top.reshape(128, 128), low.reshape(112, 128)])


def mm(a, b):
    return jnp.dot(a, b, preferred_element_type=F32)


def comm_kernel(
    ids_hbm, pos_hbm, frames_hbm, cw_hbm, w_hbm, relay_hbm, back_hbm, chan_hbm, pack_hbm, unpack_hbm,
    cot_hbm, table_hbm,
    llm_out, got_out, row_ref,
    ids_ref, pos_ref, frames, cw, wown, relay, backm, chan, pack, unpack,
    cot, table, sel_s, f_a, f_b, f_c, f_d, r_a, r_b, r_c, r_d,
    idsnd, idrcv, idcomp, idall, halo, ext, cwf, act, pooled, plo, plp,
    wpadf, wpk, wrz, wst, wfull, xs, far, opp, text, llm,
    loc_sem, halo_sem, idz_sem, idp_sem, wz_sem,
    f1_sem, f2_sem, r1_sem, r2_sem,
    ws_sem, w1_sem, wr_sem, wl_sem, pool_s, pool_r, xx_sem, xo_sem,
):
    s = lax.axis_index("seq")
    v = lax.axis_index("vocab")
    x, z, y = s // 32, (s // 4) % 8, s % 4
    p = x * 4 + y

    def at(xx, zz, yy):
        return ((xx * 8 + zz) * 4 + yy, v)

    def zpeer(d):
        return at(x, lax.rem(z + d, 8), y)

    def ppeer(j):
        return at(lax.rem(x + j // 4, 4), z, lax.rem(y + lax.rem(j, 4), 4))

    def pplace(j):
        return lax.rem(x + j // 4, 4) * 4 + lax.rem(y + lax.rem(j, 4), 4)

    nxt = (lax.rem(s + 1, N_SEQ), v)
    prv = (lax.rem(s + N_SEQ - 1, N_SEQ), v)
    other = (s, 1 - v)

    def remote(src, dst, ss, rs, dev):
        return pltpu.make_async_remote_copy(
            src_ref=src, dst_ref=dst, send_sem=ss, recv_sem=rs, device_id=dev, device_id_type=MESH
        )

    def wait_all(block, ss, rs):
        cp = remote(block, block, ss, rs, other)
        cp.wait_send()
        cp.wait_recv()

    def wait_got(block, rs):
        remote(block, block, ws_sem.at[0], rs, other).wait_recv()

    def plane(fn):
        def body(j, c):
            fn(j)
            return c

        lax.fori_loop(1, PLANE, body, 0)

    prow16 = pl.multiple_of(p * 16, 16)
    zrow = pl.multiple_of(z * 32, 32)

    def z_send(src, dst, sem, c):
        for d in (4, 3, 5, 2, 6, 1, 7):
            to = pl.multiple_of(lax.rem(z + d, 8) * 32, 32)
            remote(src.at[c, pl.ds(to, 32)], dst.at[c, pl.ds(zrow, 32)], sem.at[0, c], sem.at[1, c], zpeer(d)).start()
        dst[c, pl.ds(zrow, 32), :] = src[c, pl.ds(zrow, 32), :]

    def p_send(src, dst, sem, c):
        def send(j):
            to = pl.multiple_of(pplace(j) * 16, 16)
            remote(src.at[c, pl.ds(to, 16)], dst.at[c, pl.ds(prow16, 16)], sem.at[0, c], sem.at[1, c], ppeer(j)).start()

        plane(send)
        dst[c, pl.ds(prow16, 16), :] = src[c, pl.ds(prow16, 16), :]

    def z_wait(dst, sem, c):
        wait_all(dst.at[c, pl.ds(0, 224)], sem.at[0, c], sem.at[1, c])

    def p_wait(dst, sem, c):
        wait_all(dst.at[c, pl.ds(0, 240)], sem.at[0, c], sem.at[1, c])

    def turn(first, mid, last, sem1, sem2, c):
        p_wait(first, sem1, c)
        mid[c] = mm(backm[...], first[c]).astype(BF)
        z_send(mid, last, sem2, c)

    bar = pltpu.get_barrier_semaphore()
    for d in range(1, 8):
        pl.semaphore_signal(bar, inc=1, device_id=zpeer(d), device_id_type=MESH)
    plane(lambda j: pl.semaphore_signal(bar, inc=1, device_id=ppeer(j), device_id_type=MESH))
    for dev in (nxt, prv, other):
        pl.semaphore_signal(bar, inc=1, device_id=dev, device_id_type=MESH)

    local = {}
    for i, (name, src, dst) in enumerate(
        (
            ("ids", ids_hbm, ids_ref), ("pos", pos_hbm, pos_ref), ("w", w_hbm, wown), ("pack", pack_hbm, pack),
            ("frames", frames_hbm, frames), ("cot", cot_hbm, cot), ("relay", relay_hbm, relay), ("cw", cw_hbm, cw),
            ("unpack", unpack_hbm, unpack), ("back", back_hbm, backm), ("table", table_hbm, table),
            ("chan", chan_hbm, chan),
        )
    ):
        local[name] = pltpu.make_async_copy(src, dst, loc_sem.at[i])
        local[name].start()

    local["ids"].wait()
    local["pos"].wait()
    bcol = lax.broadcasted_iota(jnp.int32, (SLOT, 1), 0)
    bz, bk, bp = bcol >> 5, (bcol >> 4) & 1, bcol & 15
    low = (((bp >> 2) * 8 + bz) * 4 + (bp & 3)) * VROWS
    rel = ids_ref[...] - low
    qint = lax.broadcasted_iota(jnp.int32, (SLOT, SLOT), 1)
    qi = qint.astype(F32)
    hit = (rel >= 0) & (rel < VROWS)
    first = jnp.min(jnp.where(hit, qi, 4096.0), axis=1, keepdims=True)
    last = jnp.max(jnp.where(hit, qi, -1.0), axis=1, keepdims=True)
    chosen = jnp.where(bk == 0, first, jnp.where(last > first, last, -1.0))
    picked = qi == chosen
    sel_s[...] = jnp.where(picked, 1.0, 0.0).astype(BF)
    code = jnp.sum(jnp.where(picked, (qint * 2048 + rel + 1).astype(F32), 0.0), axis=1, keepdims=True)
    brow = lax.broadcasted_iota(jnp.int32, (SLOT, SLOT), 0)
    diag = brow == qint
    coderow = jnp.sum(jnp.where(diag, code, 0.0), axis=0, keepdims=True).astype(jnp.int32)
    start = pos_ref[0:1, 0:1]
    eight = lax.broadcasted_iota(jnp.int32, (8, 128), 0)
    idsnd[...] = jnp.where(
        eight == 0, coderow[:, 0:128], jnp.where(eight == 1, coderow[:, 128:256], jnp.broadcast_to(start, (8, 128)))
    )
    zrow8 = pl.multiple_of(z * 8, 8)
    idrcv[pl.ds(zrow8, 8), :] = idsnd[...]

    pl.semaphore_wait(bar, 7 + PLANE - 1 + 3)

    for d in (1, 7, 2, 6, 3, 5, 4):
        remote(idsnd, idrcv.at[pl.ds(zrow8, 8)], idz_sem.at[0], idz_sem.at[1], zpeer(d)).start()
    local["frames"].wait()
    remote(frames.at[pl.ds(FR - 16, 16)], halo.at[0], halo_sem.at[0], halo_sem.at[1], nxt).start()
    remote(frames.at[pl.ds(0, 16)], halo.at[1], halo_sem.at[0], halo_sem.at[1], prv).start()
    local["w"].wait()
    local["pack"].wait()
    wpadf[...] = jnp.zeros_like(wpadf)
    wpadf[0:WROWS, :] = wown[...].astype(F32)
    wp = wpadf[...].astype(BF)
    half = D // 2
    wpk[:, 0:half] = (mm(pack[0:16], wp[:, 0:half]) + mm(pack[16:32], wp[:, half:])).astype(BF)
    tail = jnp.zeros((16, 256), F32)
    for g in range(7):
        tail = tail + mm(pack[32 + 16 * g : 48 + 16 * g], wp[:, 256 * g : 256 * g + 256])
    wpk[:, half:] = tail.astype(BF)
    zrow16 = pl.multiple_of(z * 16, 16)
    wrz[pl.ds(zrow16, 16), :] = wpk[...]

    for d in (4, 3, 5, 2, 6, 1, 7):
        remote(wpk, wrz.at[pl.ds(zrow16, 16)], wz_sem.at[0], wz_sem.at[1], zpeer(d)).start()
    local["cot"].wait()
    local["relay"].wait()
    for c in range(NC):
        f_a[c] = mm(relay[...], mm(sel_s[...], cot[:, c * CW : (c + 1) * CW]).astype(BF)).astype(BF)
        if c == 0:
            p_send(f_a, f_b, f1_sem, 0)
    for name in ("cw", "unpack", "back", "table", "chan"):
        local[name].wait()

    wait_all(idrcv.at[pl.ds(0, 56)], idz_sem.at[0], idz_sem.at[1])
    even = idrcv[pl.ds(0, 8, stride=8), :]
    odd = idrcv[pl.ds(1, 8, stride=8), :]
    idcomp[0:8, :] = jnp.where(z < 4, even, odd)
    idcomp[8:16, :] = idrcv[pl.ds(2, 8, stride=8), :]
    idall[pl.ds(prow16, 16), :] = idcomp[...]
    plane(
        lambda j: remote(idcomp, idall.at[pl.ds(prow16, 16)], idp_sem.at[0], idp_sem.at[1], ppeer(j)).start()
    )
    p_send(f_a, f_b, f1_sem, 1)

    wait_all(halo, halo_sem.at[0], halo_sem.at[1])
    for l in range(5):
        cols = slice(128 * l, 128 * l + 128)
        ext[l, 16 : 16 + FR, :] = frames[:, cols].astype(F32)
        ext[l, 0:16, :] = jnp.where(s > 0, halo[0, :, cols].astype(F32), 0.0)
        ext[l, 16 + FR : 32 + FR, :] = jnp.where(s < N_SEQ - 1, halo[1, :, cols].astype(F32), 0.0)
        cwf[l, 0:TAPS, :] = cw[:, cols].astype(F32)

    def conv(i, carry):
        l, rb = i // 8, lax.rem(i, 8)
        r0 = pl.multiple_of(rb * 64, 64)
        acc = jnp.zeros((64, 128), F32)
        for j in range(TAPS):
            acc = acc + ext[l, pl.ds(r0 + (j + 1), 64), :] * cwf[l, pl.ds(j, 1), :]
        act[...] = ext[l, pl.ds(r0 + 16, 64), :] + acc / (1.0 + jnp.exp(-acc))
        total = act[pl.ds(0, 16, stride=4), :]
        for k in range(1, POOL):
            total = total + act[pl.ds(k, 16, stride=4), :]
        pooled[pl.ds(pl.multiple_of(rb * 16, 16), 16), pl.ds(pl.multiple_of(l * 128, 128), 128)] = (
            total * (1.0 / POOL)
        ).astype(BF)
        return carry

    lax.fori_loop(0, 20, conv, 0)

    turn(f_b, f_c, f_d, f1_sem, f2_sem, 0)
    lax.fori_loop(20, 40, conv, 0)
    plo[v] = mm(pooled[...], chan[...]).astype(BF)
    core_cp = remote(plo.at[v], plo.at[v], pool_s.at[0], pool_r.at[0], other)
    next_cp = remote(plo.at[v], plp.at[v], pool_s.at[1], pool_r.at[1], nxt)
    core_cp.start()
    next_cp.start()

    wait_all(wrz.at[pl.ds(0, 112)], wz_sem.at[0], wz_sem.at[1])
    prow80 = pl.multiple_of(p * KB, 16)
    packed = wrz[...]
    for c in range(NC):
        wst[c, 0:64, :] = mm(unpack[64 * c : 64 * c + 64], packed[:, 0:half]).astype(BF)
    for g in range(7):
        piece = mm(unpack[128 + 16 * g : 144 + 16 * g], packed[:, half:]).astype(BF)
        for b in range(2):
            col = 256 * g + 128 * b
            c, off = col // CW, col % CW
            wst[c, 64:KB, off : off + 128] = piece[:, 128 * b : 128 * b + 128]
    mine = lax.rem(x, 2)
    wfull[pl.ds(prow80, KB), :] = wst[mine]

    def wblock(f, g):
        return wfull.at[pl.ds(pl.multiple_of((lax.rem(x + f, 4) * 4 + lax.rem(y + g, 4)) * KB, 16), KB)]

    def wsend(block, dst, sem, dev):
        remote(block, dst, ws_sem.at[0], sem, dev).start()

    def wsecond(f):
        up, down = (wr_sem.at[f], wl_sem.at[0]) if f < 2 else (wl_sem.at[0], wr_sem.at[f])
        wsend(wblock(f, 0), wblock(f, 0), up, at(x, z, lax.rem(y + 1, 4)))
        wsend(wblock(f, 0), wblock(f, 0), down, at(x, z, lax.rem(y + 3, 4)))

    def w2relay(f):
        near, to = (3, 1) if f < 2 else (1, 3)
        wait_got(wblock(f, near), wr_sem.at[f])
        wsend(wblock(f, near), wblock(f, near), wl_sem.at[0], at(x, z, lax.rem(y + to, 4)))

    def xpeer(f):
        return at(lax.rem(x + f, 4), z, y)

    for f in (1, 3, 2):
        wsend(wst.at[mine if f == 2 else 1 - mine], wblock(0, 0), w1_sem.at[f], xpeer(f))
    wsecond(0)

    wait_all(idall.at[pl.ds(0, 240)], idp_sem.at[0], idp_sem.at[1])
    dup, dupst, sts = [], [], []
    for i in range(PLANE):
        piece, stp = idall[16 * i : 16 * i + 8, :], idall[16 * i + 8 : 16 * i + 16, :]
        dup += [piece, piece]
        dupst += [stp, stp]
        sts.append(stp)
    every = jnp.concatenate(dup, axis=0)
    lane = lax.broadcasted_iota(jnp.int32, (SLOT, 128), 1)
    rrow = lax.broadcasted_iota(jnp.int32, (SLOT, 128), 0)
    want = lax.rem(z, 4) * 32 + ((rrow >> 3) & 1) * 16 + p
    codes = jnp.sum(jnp.where(lane == want, every, 0).astype(F32), axis=1, keepdims=True).astype(jnp.int32)
    starts = jnp.concatenate(dupst, axis=0)[:, 0:1]
    mrow = lax.broadcasted_iota(jnp.int32, (128, 128), 0)
    mcol = lax.broadcasted_iota(jnp.int32, (128, 128), 1)
    strow = jnp.sum(
        jnp.where(mrow == mcol, jnp.concatenate(sts, axis=0).astype(F32), 0.0), axis=0, keepdims=True
    )
    rcol = lax.broadcasted_iota(jnp.int32, (SLOT, 1), 0)
    rp = rcol >> 4
    rs = ((rp >> 2) * 8 + (rcol & 7)) * 4 + (rp & 3)
    rprev = rs - 1
    prevm = jnp.where(rs == 0, -1, ((rprev >> 5) * 4 + (rprev & 3)) * 8 + ((rprev >> 2) & 7))
    prevst = jnp.sum(jnp.where(lane == prevm, strow, 0.0), axis=1, keepdims=True).astype(jnp.int32)
    prevst = jnp.where(rs == 0, -4096, prevst)
    rslot = rs * SLOT + (codes >> 11)
    audio = ((rslot >= starts) & (rslot < starts + RUN)) | ((rslot >= prevst) & (rslot < prevst + RUN))
    rowid = jnp.where(audio | (codes == 0), -1, (codes & 2047) - 1)
    vi = lax.broadcasted_iota(jnp.int32, (SLOT, VROWS), 1)
    look = jnp.where(vi == rowid, 1.0, 0.0).astype(BF)

    r_a[0] = mm(look, table[:, 0:CW]).astype(BF)
    p_send(r_a, r_b, r1_sem, 0)
    r_a[1] = mm(look, table[:, CW:]).astype(BF)

    rowrow = jnp.sum(jnp.where(diag, rowid.astype(F32), 0.0), axis=0, keepdims=True).astype(jnp.int32)
    sprev = lax.rem(s + N_SEQ - 1, N_SEQ)
    mprev = ((sprev // 32) * 4 + lax.rem(sprev, 4)) * 8 + lax.rem(sprev // 4, 8)
    mlane = lax.broadcasted_iota(jnp.int32, (1, 128), 1)
    before = jnp.sum(jnp.where(mlane == mprev, strow, 0.0), axis=1, keepdims=True).astype(jnp.int32)
    before = jnp.where(s > 0, before, -4096)

    turn(f_b, f_c, f_d, f1_sem, f2_sem, 1)
    for f in (1, 3, 2):
        wait_got(wblock(f, 0), w1_sem.at[4 - f])
        wsecond(f)

    p_send(r_a, r_b, r1_sem, 1)
    turn(r_b, r_c, r_d, r1_sem, r2_sem, 0)
    next_cp.wait()
    fwd_cp = remote(plp.at[v], plp.at[v], pool_s.at[2], pool_r.at[2], other)
    fwd_cp.start()
    w2relay(0)

    core_cp.wait()
    fwd_cp.wait()
    def xsend(src, dst, sem, f):
        remote(src, dst, sem.at[0], sem.at[1], xpeer(f)).start()

    qslot = s * SLOT + lax.broadcasted_iota(jnp.int32, (SLOT, RUN), 0)
    prun = lax.broadcasted_iota(jnp.int32, (SLOT, RUN), 1)
    own_sel = jnp.where(qslot == start + prun, 1.0, 0.0).astype(BF)
    prev_sel = jnp.where(qslot == before + prun, 1.0, 0.0).astype(BF)
    for h in range(2):
        xs[h, 0:SLOT, :] = (mm(own_sel, plo[h]) + mm(prev_sel, plp[h])).astype(BF)
    xsend(xs.at[v, pl.ds(0, RUN)], xs.at[v, pl.ds(SLOT, RUN)], xx_sem, 1)
    xsend(xs.at[v, pl.ds(RUN, RUN)], xs.at[v, pl.ds(SLOT + RUN, RUN)], xx_sem, 3)

    turn(r_b, r_c, r_d, r1_sem, r2_sem, 1)
    for f in (1, 3, 2):
        w2relay(f)

    wait_all(xs.at[v, pl.ds(SLOT, SLOT)], xx_sem.at[0], xx_sem.at[1])
    x_cp = remote(xs.at[v, pl.ds(SLOT, SLOT)], xs.at[v, pl.ds(SLOT, SLOT)], pool_s.at[3], pool_r.at[3], other)
    x_cp.start()

    for c in range(NC):
        z_wait(f_d, f2_sem, c)
    got_cps = []
    for c in range(NC):
        f_c[c] = mm(relay[...], f_d[c]).astype(BF)
        got_cps.append(pltpu.make_async_copy(f_c.at[c], got_out.at[:, pl.ds(c * CW, CW)], loc_sem.at[2 + c]))
        got_cps[-1].start()
    row_ref[...] = jnp.broadcast_to(rowrow, (8, SLOT))
    x_cp.wait()
    wait_got(wfull.at[pl.ds(0, 8 * KB)], wl_sem.at[0])
    far[...] = (mm(xs[0, SLOT:, :], wfull[0:CH, :]) + mm(xs[1, SLOT:, :], wfull[CH:, :])).astype(BF)
    xsend(far.at[pl.ds(0, RUN)], opp.at[pl.ds(0, RUN)], xo_sem, 3)
    xsend(far.at[pl.ds(RUN, RUN)], opp.at[pl.ds(RUN, RUN)], xo_sem, 1)
    near = mm(xs[0, 0:SLOT, :], wfull[0:CH, :]) + mm(xs[1, 0:SLOT, :], wfull[CH:, :])
    near = near.astype(BF).astype(F32)
    for c in range(NC):
        z_wait(r_d, r2_sem, c)
        text[c] = lax.dot_general(
            sel_s[...], r_d[c], (((0,), (0,)), ((), ())), preferred_element_type=F32
        ).astype(BF)
    llm[mine] = (near + text[mine].astype(F32)).astype(BF)
    outs = [pltpu.make_async_copy(llm.at[mine], llm_out.at[mine], loc_sem.at[0])]
    outs[0].start()
    wait_all(opp, xo_sem.at[0], xo_sem.at[1])
    llm[1 - mine] = (opp[...].astype(F32) + text[1 - mine].astype(F32)).astype(BF)
    outs.append(pltpu.make_async_copy(llm.at[1 - mine], llm_out.at[1 - mine], loc_sem.at[1]))
    outs[1].start()
    block = wfull.at[pl.ds(0, 15 * KB)]
    remote(block, block, ws_sem.at[0], wl_sem.at[0], other).wait_send()
    for cp in got_cps:
        cp.wait()
    for cp in outs:
        cp.wait()


def write_kernel(row_hbm, got_hbm, llm_hbm, out_hbm, grad_hbm, row, got, llm, grad, in_sem, out_sem):
    tiles = D // TILE
    row_cp = pltpu.make_async_copy(row_hbm, row, in_sem.at[tiles])
    row_cp.start()
    ins = []
    for i in range(tiles):
        ins.append(pltpu.make_async_copy(got_hbm.at[:, pl.ds(i * TILE, TILE)], got.at[i], in_sem.at[i]))
        ins[-1].start()
    llm_in = pltpu.make_async_copy(llm_hbm, llm, in_sem.at[tiles + 1])
    llm_in.start()
    row_cp.wait()
    vi = lax.broadcasted_iota(jnp.int32, (VROWS, SLOT), 0)
    place = jnp.where(vi == row[0:1, :], 1.0, 0.0).astype(BF)
    outs = []
    for i in range(tiles):
        ins[i].wait()
        grad[i] = mm(place, got[i]).astype(BF)
        outs.append(pltpu.make_async_copy(grad.at[i], grad_hbm.at[:, pl.ds(i * TILE, TILE)], out_sem.at[i]))
        outs[-1].start()
    llm_in.wait()
    for h in range(NC):
        outs.append(pltpu.make_async_copy(llm.at[h], out_hbm.at[:, pl.ds(h * CW, CW)], out_sem.at[tiles + h]))
        outs[-1].start()
    for cp in outs:
        cp.wait()


def shards(frames, conv_weight, proj_weight, table, audio_pos, token_ids, cotangent):
    relay = relay_matrix()
    consts = [relay, relay.T, channel_matrix(), pack_matrices(), unpack_matrices()]
    consts = [jnp.asarray(m, dtype=BF) for m in consts]
    hbm = pl.BlockSpec(memory_space=pltpu.HBM)
    anywhere = pl.BlockSpec(memory_space=pl.ANY)
    dma = pltpu.SemaphoreType.DMA
    wide = pltpu.VMEM((NC, SLOT, CW), BF)
    llm, got, rows = pl.pallas_call(
        comm_kernel,
        out_shape=[
            jax.ShapeDtypeStruct((NC, SLOT, CW), BF),
            jax.ShapeDtypeStruct((SLOT, D), BF),
            jax.ShapeDtypeStruct((8, SLOT), jnp.int32),
        ],
        in_specs=[hbm] * 12,
        out_specs=[anywhere, anywhere, pl.BlockSpec(memory_space=pltpu.VMEM)],
        scratch_shapes=[
            pltpu.VMEM((1, SLOT), jnp.int32),
            pltpu.VMEM((1, RUN), jnp.int32),
            pltpu.VMEM((FR, CH), BF),
            pltpu.VMEM((TAPS, CH), BF),
            pltpu.VMEM((WROWS, D), BF),
            pltpu.VMEM((SLOT, SLOT), BF),
            pltpu.VMEM((SLOT, SLOT), BF),
            pltpu.VMEM((CH, CH), BF),
            pltpu.VMEM((144, 16), BF),
            pltpu.VMEM((240, 128), BF),
            pltpu.VMEM((SLOT, D), BF),
            pltpu.VMEM((VROWS, D), BF),
            pltpu.VMEM((SLOT, SLOT), BF),
            wide, wide, wide, wide, wide, wide, wide, wide,
            pltpu.VMEM((8, 128), jnp.int32),
            pltpu.VMEM((64, 128), jnp.int32),
            pltpu.VMEM((16, 128), jnp.int32),
            pltpu.VMEM((256, 128), jnp.int32),
            pltpu.VMEM((2, 16, CH), BF),
            pltpu.VMEM((5, FR + 32, 128), F32),
            pltpu.VMEM((5, 32, 128), F32),
            pltpu.VMEM((64, 128), F32),
            pltpu.VMEM((RUN, CH), BF),
            pltpu.VMEM((2, RUN, CH), BF),
            pltpu.VMEM((2, RUN, CH), BF),
            pltpu.VMEM((16, D), F32),
            pltpu.VMEM((16, WP), BF),
            pltpu.VMEM((128, WP), BF),
            pltpu.VMEM((NC, KB, CW), BF),
            pltpu.VMEM((PLANE * KB, CW), BF),
            pltpu.VMEM((2, 2 * SLOT, CH), BF),
            pltpu.VMEM((SLOT, CW), BF),
            pltpu.VMEM((SLOT, CW), BF),
            wide, wide,
            dma((12,)), dma((2,)), dma((2,)), dma((2,)), dma((2,)),
            dma((2, 2)), dma((2, 2)), dma((2, 2)), dma((2, 2)),
            dma((1,)), dma((4,)), dma((4,)), dma((1,)), dma((4,)), dma((4,)), dma((2,)), dma((2,)),
        ],
        compiler_params=pltpu.CompilerParams(
            collective_id=0, has_side_effects=True, vmem_limit_bytes=VMEM_LIMIT
        ),
        name="exchange",
    )(
        token_ids.reshape(1, SLOT), audio_pos.reshape(1, RUN), frames, conv_weight, proj_weight, *consts,
        cotangent, table,
    )
    return pl.pallas_call(
        write_kernel,
        out_shape=[jax.ShapeDtypeStruct((SLOT, D), BF), jax.ShapeDtypeStruct((VROWS, D), BF)],
        in_specs=[hbm] * 3,
        out_specs=[anywhere, anywhere],
        scratch_shapes=[
            pltpu.VMEM((8, SLOT), jnp.int32),
            pltpu.VMEM((D // TILE, SLOT, TILE), BF),
            wide,
            pltpu.VMEM((D // TILE, VROWS, TILE), BF),
            dma((D // TILE + 2,)),
            dma((D // TILE + 2,)),
        ],
        compiler_params=pltpu.CompilerParams(vmem_limit_bytes=VMEM_LIMIT),
        name="write",
    )(rows, got, llm)


def solution(mesh):
    return jax.shard_map(
        shards,
        mesh=mesh,
        in_specs=(
            P("seq", "vocab"),
            P(None, "vocab"),
            P("seq", "vocab"),
            P("seq", "vocab"),
            P("seq"),
            P("seq"),
            P("seq", "vocab"),
        ),
        out_specs=(P("seq", "vocab"), P("seq", "vocab")),
        check_vma=False,
    )
```

time: 191 us -> 72.4 us (0.38)
  Pallas kernels: 0 us -> 70.8 us
  waiting for transfers between devices: 54 us -> 0 us
  starting transfers between devices: 47.6 us -> 0 us
  other arithmetic: 38.4 us -> 0 us
  local copies, waits for them, and re-layouts: 29.1 us -> 0 us
  between operations: 14.9 us -> 0.64 us
  matrix products: 3.17 us -> 0 us
  blocking collectives: 2.04 us -> 0 us
    pallas_call x0 -> x2, Pallas kernels: none -> 70.8 us  [the longest x1 65.4 us: shards(): pl.pallas_call(comm_kernel, out_shape=[jax.ShapeDtypeStruct((NC, SLOT, CW...]
    all_to_all x3 -> x0, starting transfers between devices: 29.8 us -> none  [the longest x1 12.6 us: shards(): lax.all_to_all(send_ids, 'seq', split_axis=0, concat_axis=0, tiled=True)]
    all_gather x1 -> x0, waiting for transfers between devices: 28.5 us -> none  [project(): lax.all_gather(proj_weight, 'seq', axis=0, tiled=True)]
    all_to_all x3 -> x0, waiting for transfers between devices: 24.8 us -> none  [the longest x1 18.9 us: shards(): lax.all_to_all(send_grad, 'seq', split_axis=0, concat_axis=0, tiled=True)]
    ppermute x4 -> x0, starting transfers between devices: 17.7 us -> none  [the longest x1 8.61 us: extended(): after = lax.ppermute(first, axis, down)]
    add x1 -> x0, other arithmetic: 12.9 us -> none  [shards(): activated = frames.astype(jnp.float32) + jax.nn.silu(filtered)]
    unnamed x84 -> x0, local copies, waits for them, and re-layouts: 9.57 us -> none
    scatter-add x1 -> x0, other arithmetic: 7.21 us -> none  [shards(): gradient = jnp.zeros((run_rows, feature_count), jnp.float32).at[local_row...]
  transfers between devices with their start and end apart: 8 -> 0, of which waited for: 3 -> 0; matrix products, arithmetic and copies ran while one was open for 35% -> 0% of each run, Pallas kernels for 0% -> 0%
where the time goes in v2:
time: 72.4 us; the launch traced here: 71.4 us
  Pallas kernels  70.8 us (98%)
    pallas_call x1, Pallas kernels, shards(): pl.pallas_call(comm_kernel, out_shape=[jax.ShapeDtypeStruct((NC, SLOT, CW...  65.4 us
    pallas_call x1, Pallas kernels, shards(): pl.pallas_call(write_kernel, out_shape=[jax.ShapeDtypeStruct((SLOT, D), B...  5.32 us

profile of v2, /device:TPU:2, one launch (start us, length us, event | category | flops | bytes accessed | tf_op | source)
XLA Modules:
  0.0 71.4 jit_solution(141005667432988870)
XLA Ops:
  0.6 65.4 %exchange.1 = (bf16[2,256,896]{2,1,0:T(8,128)(2,1)}, bf16[256,1792]{1,0:T(8,128)(2,1)}, s32[8,256]{1,0:T(8,128)}) custom-call(s32[1,256]{1,0:T(1,128)} %bitcast.2, s32[1,128]{1,0:T(1,128)} %bitcast.3, bf16[512,640]{1,0:T(8,128)(2,1)} %frames_hbm.1, bf16[31,640]{1,0:T(8,128)(2,1)} %cw_hbm.1, bf16[10,1792]{1,0:T(8,128)(2,1)} %w_hbm.1, ...), custom_call_target="tpu_custom_call" | custom-call | tf_op jit(solution)/shard_map/exchange/pallas_call | solution.py:465
  66.1 5.3 %write.1 = (bf16[256,1792]{1,0:T(8,128)(2,1)}, bf16[1188,1792]{1,0:T(8,128)(2,1)}) custom-call(s32[8,256]{1,0:T(8,128)} %get-tuple-element.5.row_hbm, bf16[256,1792]{1,0:T(8,128)(2,1)} %get-tuple-element.6.got_hbm, bf16[2,256,896]{2,1,0:T(8,128)(2,1)} %get-tuple-element.7.llm_hbm), custom_call_target="tpu_custom_call" | custom-call | tf_op jit(solution)/shard_map/write/pallas_call | solution.py:521

commit v3 on v2

--- a/solution.py
+++ b/solution.py
@@ -17,10 +17,13 @@
 POOL = 4
 SLOT = 256
 RUN = 128
+PART = 32
 VROWS = 1188
 D = 1792
 NC = 2
 CW = D // NC
+WHOLE = (0, CW)
+EARLY = ((0, 384, 0), (384, 512, 1))
 CH = 640
 FR = 512
 TAPS = 31
@@ -84,7 +87,7 @@
     ids_ref, pos_ref, frames, cw, wown, relay, backm, chan, pack, unpack,
     cot, table, sel_s, f_a, f_b, f_c, f_d, r_a, r_b, r_c, r_d,
     idsnd, idrcv, idcomp, idall, halo, ext, cwf, act, pooled, plo, plp,
-    wpadf, wpk, wrz, wst, wfull, xs, far, opp, text, llm,
+    wpadf, wpk, wrz, wst, wfull, xs, far, opp, text, llm, passing,
     loc_sem, halo_sem, idz_sem, idp_sem, wz_sem,
     f1_sem, f2_sem, r1_sem, r2_sem,
     ws_sem, w1_sem, wr_sem, wl_sem, pool_s, pool_r, xx_sem, xo_sem,
@@ -109,6 +112,11 @@
     nxt = (lax.rem(s + 1, N_SEQ), v)
     prv = (lax.rem(s + N_SEQ - 1, N_SEQ), v)
     other = (s, 1 - v)
+    ahead = (lax.rem((s // 4 + 1) * 4, N_SEQ), v)
+
+    def behind(i):
+        return (lax.rem(s + N_SEQ - 4 + i, N_SEQ), v)
+
 
     def remote(src, dst, ss, rs, dev):
         return pltpu.make_async_remote_copy(
@@ -133,37 +141,51 @@
     prow16 = pl.multiple_of(p * 16, 16)
     zrow = pl.multiple_of(z * 32, 32)
 
-    def z_send(src, dst, sem, c):
+    def z_send(src, dst, sem, c, part=WHOLE):
+        cols = pl.ds(part[0], part[1])
         for d in (4, 3, 5, 2, 6, 1, 7):
             to = pl.multiple_of(lax.rem(z + d, 8) * 32, 32)
-            remote(src.at[c, pl.ds(to, 32)], dst.at[c, pl.ds(zrow, 32)], sem.at[0, c], sem.at[1, c], zpeer(d)).start()
-        dst[c, pl.ds(zrow, 32), :] = src[c, pl.ds(zrow, 32), :]
-
-    def p_send(src, dst, sem, c):
+            remote(
+                src.at[c, pl.ds(to, 32), cols], dst.at[c, pl.ds(zrow, 32), cols], sem.at[0, c], sem.at[1, c], zpeer(d)
+            ).start()
+        dst[c, pl.ds(zrow, 32), cols] = src[c, pl.ds(zrow, 32), cols]
+
+    def p_send(src, dst, sem, c, part=WHOLE):
+        cols = pl.ds(part[0], part[1])
+
         def send(j):
             to = pl.multiple_of(pplace(j) * 16, 16)
-            remote(src.at[c, pl.ds(to, 16)], dst.at[c, pl.ds(prow16, 16)], sem.at[0, c], sem.at[1, c], ppeer(j)).start()
+            remote(
+                src.at[c, pl.ds(to, 16), cols], dst.at[c, pl.ds(prow16, 16), cols], sem.at[0, c], sem.at[1, c], ppeer(j)
+            ).start()
 
         plane(send)
-        dst[c, pl.ds(prow16, 16), :] = src[c, pl.ds(prow16, 16), :]
+        dst[c, pl.ds(prow16, 16), cols] = src[c, pl.ds(prow16, 16), cols]
 
     def z_wait(dst, sem, c):
         wait_all(dst.at[c, pl.ds(0, 224)], sem.at[0, c], sem.at[1, c])
 
-    def p_wait(dst, sem, c):
-        wait_all(dst.at[c, pl.ds(0, 240)], sem.at[0, c], sem.at[1, c])
-
-    def turn(first, mid, last, sem1, sem2, c):
-        p_wait(first, sem1, c)
-        mid[c] = mm(backm[...], first[c]).astype(BF)
-        z_send(mid, last, sem2, c)
+    def p_wait(dst, sem, c, part=WHOLE):
+        wait_all(dst.at[c, pl.ds(0, 240), pl.ds(part[0], part[1])], sem.at[0, c], sem.at[1, c])
+
+    def turn(first, mid, last, sem1, sem2, c, part=WHOLE):
+        cols = pl.ds(part[0], part[1])
+        p_wait(first, sem1, c, part)
+        mid[c, :, cols] = mm(backm[...], first[c, :, cols]).astype(BF)
+        z_send(mid, last, sem2, c, part)
 
     bar = pltpu.get_barrier_semaphore()
     for d in range(1, 8):
         pl.semaphore_signal(bar, inc=1, device_id=zpeer(d), device_id_type=MESH)
     plane(lambda j: pl.semaphore_signal(bar, inc=1, device_id=ppeer(j), device_id_type=MESH))
-    for dev in (nxt, prv, other):
+    for dev in (nxt, prv, other, ahead):
         pl.semaphore_signal(bar, inc=1, device_id=dev, device_id_type=MESH)
+
+    @pl.when(y == 0)
+    def _():
+        for i in range(4):
+            pl.semaphore_signal(bar, inc=1, device_id=behind(i), device_id_type=MESH)
+
 
     local = {}
     for i, (name, src, dst) in enumerate(
@@ -203,13 +225,6 @@
     zrow8 = pl.multiple_of(z * 8, 8)
     idrcv[pl.ds(zrow8, 8), :] = idsnd[...]
 
-    pl.semaphore_wait(bar, 7 + PLANE - 1 + 3)
-
-    for d in (1, 7, 2, 6, 3, 5, 4):
-        remote(idsnd, idrcv.at[pl.ds(zrow8, 8)], idz_sem.at[0], idz_sem.at[1], zpeer(d)).start()
-    local["frames"].wait()
-    remote(frames.at[pl.ds(FR - 16, 16)], halo.at[0], halo_sem.at[0], halo_sem.at[1], nxt).start()
-    remote(frames.at[pl.ds(0, 16)], halo.at[1], halo_sem.at[0], halo_sem.at[1], prv).start()
     local["w"].wait()
     local["pack"].wait()
     wpadf[...] = jnp.zeros_like(wpadf)
@@ -224,28 +239,57 @@
     zrow16 = pl.multiple_of(z * 16, 16)
     wrz[pl.ds(zrow16, 16), :] = wpk[...]
 
-    for d in (4, 3, 5, 2, 6, 1, 7):
-        remote(wpk, wrz.at[pl.ds(zrow16, 16)], wz_sem.at[0], wz_sem.at[1], zpeer(d)).start()
     local["cot"].wait()
     local["relay"].wait()
-    for c in range(NC):
+
+    def bucketed(c):
         f_a[c] = mm(relay[...], mm(sel_s[...], cot[:, c * CW : (c + 1) * CW]).astype(BF)).astype(BF)
-        if c == 0:
-            p_send(f_a, f_b, f1_sem, 0)
+
+    bucketed(0)
+    local["frames"].wait()
+
+    @pl.when(y == 0)
+    def _():
+        pl.semaphore_wait(bar, 7 + PLANE - 1 + 8)
+
+    @pl.when(y > 0)
+    def _():
+        pl.semaphore_wait(bar, 7 + PLANE - 1 + 4)
+
+
+    for d in (1, 7, 2, 6, 3, 5, 4):
+        remote(idsnd, idrcv.at[pl.ds(zrow8, 8)], idz_sem.at[0], idz_sem.at[1], zpeer(d)).start()
+    remote(frames.at[pl.ds(FR - 16, 16)], halo.at[0], halo_sem.at[0], halo_sem.at[1], nxt).start()
+    remote(frames.at[pl.ds(0, 16)], halo.at[1], halo_sem.at[0], halo_sem.at[1], prv).start()
+    def ring_block(k):
+        return wrz.at[pl.ds(pl.multiple_of(lax.rem(z + k, 8) * 16, 16), 16)]
+
+    for d in (2, 6, 1, 7):
+        remote(wpk, ring_block(0), wz_sem.at[0], wz_sem.at[1 if d in (1, 7) else d], zpeer(d)).start()
+    for part in EARLY:
+        p_send(f_a, f_b, f1_sem.at[part[2]], 0, part)
+    bucketed(1)
     for name in ("cw", "unpack", "back", "table", "chan"):
         local[name].wait()
 
     wait_all(idrcv.at[pl.ds(0, 56)], idz_sem.at[0], idz_sem.at[1])
     even = idrcv[pl.ds(0, 8, stride=8), :]
     odd = idrcv[pl.ds(1, 8, stride=8), :]
-    idcomp[0:8, :] = jnp.where(z < 4, even, odd)
-    idcomp[8:16, :] = idrcv[pl.ds(2, 8, stride=8), :]
-    idall[pl.ds(prow16, 16), :] = idcomp[...]
+    lane8 = lax.broadcasted_iota(jnp.int32, (8, 128), 1)
+    at_start = lax.rem(z + 1, 4) * 32
+    idcomp[...] = jnp.where(lane8 == at_start, idrcv[pl.ds(2, 8, stride=8), :], jnp.where(z < 4, even, odd))
+    prow8 = pl.multiple_of(p * 8, 8)
+    idall[pl.ds(prow8, 8), :] = idcomp[...]
     plane(
-        lambda j: remote(idcomp, idall.at[pl.ds(prow16, 16)], idp_sem.at[0], idp_sem.at[1], ppeer(j)).start()
+        lambda j: remote(idcomp, idall.at[pl.ds(prow8, 8)], idp_sem.at[0], idp_sem.at[1], ppeer(j)).start()
     )
-    p_send(f_a, f_b, f1_sem, 1)
-
+    p_send(f_a, f_b, f1_sem.at[0], 1)
+
+    wait_got(ring_block(6), wz_sem.at[2])
+    remote(ring_block(6), ring_block(6), wz_sem.at[0], wz_sem.at[1], zpeer(1)).start()
+    remote(ring_block(6), ring_block(6), wz_sem.at[0], wz_sem.at[1], zpeer(2)).start()
+    wait_got(ring_block(2), wz_sem.at[6])
+    remote(ring_block(2), ring_block(2), wz_sem.at[0], wz_sem.at[1], zpeer(7)).start()
     wait_all(halo, halo_sem.at[0], halo_sem.at[1])
     for l in range(5):
         cols = slice(128 * l, 128 * l + 128)
@@ -271,15 +315,29 @@
 
     lax.fori_loop(0, 20, conv, 0)
 
-    turn(f_b, f_c, f_d, f1_sem, f2_sem, 0)
+    for part in EARLY:
+        turn(f_b, f_c, f_d, f1_sem.at[part[2]], f2_sem, 0, part)
     lax.fori_loop(20, 40, conv, 0)
     plo[v] = mm(pooled[...], chan[...]).astype(BF)
     core_cp = remote(plo.at[v], plo.at[v], pool_s.at[0], pool_r.at[0], other)
     next_cp = remote(plo.at[v], plp.at[v], pool_s.at[1], pool_r.at[1], nxt)
     core_cp.start()
-    next_cp.start()
-
-    wait_all(wrz.at[pl.ds(0, 112)], wz_sem.at[0], wz_sem.at[1])
+
+    @pl.when(y < 3)
+    def _():
+        next_cp.start()
+
+    @pl.when(y == 3)
+    def _():
+        last = pl.ds(3 * PART, PART)
+        remote(plo.at[v, last], plp.at[v, last], pool_s.at[1], pool_r.at[1], ahead).start()
+        for i in range(3):
+            remote(plo.at[v, pl.ds(i * PART, PART)], passing, pool_s.at[1], pool_r.at[4], at(x, z, i)).start()
+
+
+    wait_got(wrz.at[pl.ds(0, 80)], wz_sem.at[1])
+    sent = wrz.at[pl.ds(0, 112)]
+    remote(sent, sent, wz_sem.at[0], wz_sem.at[1], other).wait_send()
     prow80 = pl.multiple_of(p * KB, 16)
     packed = wrz[...]
     for c in range(NC):
@@ -316,24 +374,21 @@
         wsend(wst.at[mine if f == 2 else 1 - mine], wblock(0, 0), w1_sem.at[f], xpeer(f))
     wsecond(0)
 
-    wait_all(idall.at[pl.ds(0, 240)], idp_sem.at[0], idp_sem.at[1])
-    dup, dupst, sts = [], [], []
+    wait_all(idall.at[pl.ds(0, 120)], idp_sem.at[0], idp_sem.at[1])
+    dup = []
     for i in range(PLANE):
-        piece, stp = idall[16 * i : 16 * i + 8, :], idall[16 * i + 8 : 16 * i + 16, :]
+        piece = idall[8 * i : 8 * i + 8, :]
         dup += [piece, piece]
-        dupst += [stp, stp]
-        sts.append(stp)
     every = jnp.concatenate(dup, axis=0)
     lane = lax.broadcasted_iota(jnp.int32, (SLOT, 128), 1)
     rrow = lax.broadcasted_iota(jnp.int32, (SLOT, 128), 0)
     want = lax.rem(z, 4) * 32 + ((rrow >> 3) & 1) * 16 + p
     codes = jnp.sum(jnp.where(lane == want, every, 0).astype(F32), axis=1, keepdims=True).astype(jnp.int32)
-    starts = jnp.concatenate(dupst, axis=0)[:, 0:1]
+    starts = jnp.sum(jnp.where(lane == at_start, every, 0).astype(F32), axis=1, keepdims=True).astype(jnp.int32)
     mrow = lax.broadcasted_iota(jnp.int32, (128, 128), 0)
     mcol = lax.broadcasted_iota(jnp.int32, (128, 128), 1)
-    strow = jnp.sum(
-        jnp.where(mrow == mcol, jnp.concatenate(sts, axis=0).astype(F32), 0.0), axis=0, keepdims=True
-    )
+    stcol = jnp.sum(jnp.where(mcol == at_start, idall[...], 0).astype(F32), axis=1, keepdims=True)
+    strow = jnp.sum(jnp.where(mrow == mcol, stcol, 0.0), axis=0, keepdims=True)
     rcol = lax.broadcasted_iota(jnp.int32, (SLOT, 1), 0)
     rp = rcol >> 4
     rs = ((rp >> 2) * 8 + (rcol & 7)) * 4 + (rp & 3)
@@ -358,12 +413,18 @@
     before = jnp.sum(jnp.where(mlane == mprev, strow, 0.0), axis=1, keepdims=True).astype(jnp.int32)
     before = jnp.where(s > 0, before, -4096)
 
-    turn(f_b, f_c, f_d, f1_sem, f2_sem, 1)
+    p_send(r_a, r_b, r1_sem, 1)
+    @pl.when(y < 3)
+    def _():
+        part = pl.ds(pl.multiple_of(y * PART, PART), PART)
+        wait_got(passing, pool_r.at[4])
+        remote(passing, plp.at[v, part], pool_s.at[4], pool_r.at[1], ahead).start()
+
+    turn(f_b, f_c, f_d, f1_sem.at[0], f2_sem, 1)
     for f in (1, 3, 2):
         wait_got(wblock(f, 0), w1_sem.at[4 - f])
         wsecond(f)
 
-    p_send(r_a, r_b, r1_sem, 1)
     turn(r_b, r_c, r_d, r1_sem, r2_sem, 0)
     next_cp.wait()
     fwd_cp = remote(plp.at[v], plp.at[v], pool_s.at[2], pool_r.at[2], other)
@@ -419,6 +480,10 @@
     llm[1 - mine] = (opp[...].astype(F32) + text[1 - mine].astype(F32)).astype(BF)
     outs.append(pltpu.make_async_copy(llm.at[1 - mine], llm_out.at[1 - mine], loc_sem.at[1]))
     outs[1].start()
+    @pl.when(y < 3)
+    def _():
+        remote(passing, passing, pool_s.at[4], pool_r.at[4], other).wait_send()
+
     block = wfull.at[pl.ds(0, 15 * KB)]
     remote(block, block, ws_sem.at[0], wl_sem.at[0], other).wait_send()
     for cp in got_cps:
@@ -427,31 +492,44 @@
         cp.wait()
 
 
-def write_kernel(row_hbm, got_hbm, llm_hbm, out_hbm, grad_hbm, row, got, llm, grad, in_sem, out_sem):
+def write_kernel(row_hbm, got_hbm, llm_hbm, out_hbm, grad_hbm, row, got, llm, grad, place, in_sem, out_sem):
     tiles = D // TILE
+
+    def get(i):
+        cols = pl.ds(pl.multiple_of(i * TILE, TILE), TILE)
+        return pltpu.make_async_copy(got_hbm.at[:, cols], got.at[i], in_sem.at[i])
+
+    def put(i):
+        cols = pl.ds(pl.multiple_of(i * TILE, TILE), TILE)
+        return pltpu.make_async_copy(grad.at[i], grad_hbm.at[:, cols], out_sem.at[i])
+
+    def put_llm(h):
+        return pltpu.make_async_copy(llm.at[h], out_hbm.at[:, pl.ds(h * CW, CW)], out_sem.at[tiles + h])
+
     row_cp = pltpu.make_async_copy(row_hbm, row, in_sem.at[tiles])
     row_cp.start()
-    ins = []
+    llm_in = pltpu.make_async_copy(llm_hbm, llm, in_sem.at[tiles + 1])
     for i in range(tiles):
-        ins.append(pltpu.make_async_copy(got_hbm.at[:, pl.ds(i * TILE, TILE)], got.at[i], in_sem.at[i]))
-        ins[-1].start()
-    llm_in = pltpu.make_async_copy(llm_hbm, llm, in_sem.at[tiles + 1])
+        get(i).start()
     llm_in.start()
     row_cp.wait()
     vi = lax.broadcasted_iota(jnp.int32, (VROWS, SLOT), 0)
-    place = jnp.where(vi == row[0:1, :], 1.0, 0.0).astype(BF)
-    outs = []
-    for i in range(tiles):
-        ins[i].wait()
-        grad[i] = mm(place, got[i]).astype(BF)
-        outs.append(pltpu.make_async_copy(grad.at[i], grad_hbm.at[:, pl.ds(i * TILE, TILE)], out_sem.at[i]))
-        outs[-1].start()
+    place[...] = jnp.where(vi == row[0:1, :], 1.0, 0.0).astype(BF)
+
+    def tile(i, c):
+        get(i).wait()
+        grad[i] = mm(place[...], got[i]).astype(BF)
+        put(i).start()
+        return c
+
+    lax.fori_loop(0, tiles, tile, 0)
     llm_in.wait()
     for h in range(NC):
-        outs.append(pltpu.make_async_copy(llm.at[h], out_hbm.at[:, pl.ds(h * CW, CW)], out_sem.at[tiles + h]))
-        outs[-1].start()
-    for cp in outs:
-        cp.wait()
+        put_llm(h).start()
+    for i in range(tiles):
+        put(i).wait()
+    for h in range(NC):
+        put_llm(h).wait()
 
 
 def shards(frames, conv_weight, proj_weight, table, audio_pos, token_ids, cotangent):
@@ -488,8 +566,8 @@
             wide, wide, wide, wide, wide, wide, wide, wide,
             pltpu.VMEM((8, 128), jnp.int32),
             pltpu.VMEM((64, 128), jnp.int32),
-            pltpu.VMEM((16, 128), jnp.int32),
-            pltpu.VMEM((256, 128), jnp.int32),
+            pltpu.VMEM((8, 128), jnp.int32),
+            pltpu.VMEM((128, 128), jnp.int32),
             pltpu.VMEM((2, 16, CH), BF),
             pltpu.VMEM((5, FR + 32, 128), F32),
             pltpu.VMEM((5, 32, 128), F32),
@@ -506,9 +584,10 @@
             pltpu.VMEM((SLOT, CW), BF),
             pltpu.VMEM((SLOT, CW), BF),
             wide, wide,
-            dma((12,)), dma((2,)), dma((2,)), dma((2,)), dma((2,)),
-            dma((2, 2)), dma((2, 2)), dma((2, 2)), dma((2, 2)),
-            dma((1,)), dma((4,)), dma((4,)), dma((1,)), dma((4,)), dma((4,)), dma((2,)), dma((2,)),
+            pltpu.VMEM((PART, CH), BF),
+            dma((12,)), dma((2,)), dma((2,)), dma((2,)), dma((7,)),
+            dma((2, 2, 2)), dma((2, 2)), dma((2, 2)), dma((2, 2)),
+            dma((1,)), dma((4,)), dma((4,)), dma((1,)), dma((5,)), dma((5,)), dma((2,)), dma((2,)),
         ],
         compiler_params=pltpu.CompilerParams(
             collective_id=0, has_side_effects=True, vmem_limit_bytes=VMEM_LIMIT
@@ -528,6 +607,7 @@
             pltpu.VMEM((D // TILE, SLOT, TILE), BF),
             wide,
             pltpu.VMEM((D // TILE, VROWS, TILE), BF),
+            pltpu.VMEM((VROWS, SLOT), BF),
             dma((D // TILE + 2,)),
             dma((D // TILE + 2,)),
         ],

time: 72.4 us -> 69.6 us (0.961)
  Pallas kernels: 70.8 us -> 67.7 us
    pallas_call x1, Pallas kernels: 65.4 us -> 63.3 us  [shards(): pl.pallas_call(comm_kernel, out_shape=[jax.ShapeDtypeStruct((NC, SLOT, CW...]
    pallas_call x1, Pallas kernels: 5.32 us -> 4.48 us  [shards(): pl.pallas_call(write_kernel, out_shape=[jax.ShapeDtypeStruct((SLOT, D), B...]
where the time goes in v3:
time: 69.6 us; the launch traced here: 68.4 us
  Pallas kernels  67.7 us (97%)
    pallas_call x1, Pallas kernels, shards(): pl.pallas_call(comm_kernel, out_shape=[jax.ShapeDtypeStruct((NC, SLOT, CW...  63.3 us
    pallas_call x1, Pallas kernels, shards(): pl.pallas_call(write_kernel, out_shape=[jax.ShapeDtypeStruct((SLOT, D), B...  4.48 us

profile of v3, /device:TPU:2, one launch (start us, length us, event | category | flops | bytes accessed | tf_op | source)
XLA Modules:
  0.0 68.4 jit_solution(7363410353545103740)
XLA Ops:
  0.6 63.3 %exchange.1 = (bf16[2,256,896]{2,1,0:T(8,128)(2,1)}, bf16[256,1792]{1,0:T(8,128)(2,1)}, s32[8,256]{1,0:T(8,128)}) custom-call(s32[1,256]{1,0:T(1,128)} %bitcast.2, s32[1,128]{1,0:T(1,128)} %bitcast.3, bf16[512,640]{1,0:T(8,128)(2,1)} %frames_hbm.1, bf16[31,640]{1,0:T(8,128)(2,1)} %cw_hbm.1, bf16[10,1792]{1,0:T(8,128)(2,1)} %w_hbm.1, ...), custom_call_target="tpu_custom_call" | custom-call | tf_op jit(solution)/shard_map/exchange/pallas_call | solution.py:543
  63.9 4.5 %write.1 = (bf16[256,1792]{1,0:T(8,128)(2,1)}, bf16[1188,1792]{1,0:T(8,128)(2,1)}) custom-call(s32[8,256]{1,0:T(8,128)} %get-tuple-element.5.row_hbm, bf16[256,1792]{1,0:T(8,128)(2,1)} %get-tuple-element.6.got_hbm, bf16[2,256,896]{2,1,0:T(8,128)(2,1)} %get-tuple-element.7.llm_hbm), custom_call_target="tpu_custom_call" | custom-call | tf_op jit(solution)/shard_map/write/pallas_call | solution.py:600

commit v4 on v3

--- a/solution.py
+++ b/solution.py
@@ -31,6 +31,7 @@
 WP = 1152
 KB = NZ * WROWS
 TILE = 256
+PRE = 3
 VMEM_LIMIT = 60 * 1024 * 1024
 
 
@@ -83,11 +84,11 @@
 def comm_kernel(
     ids_hbm, pos_hbm, frames_hbm, cw_hbm, w_hbm, relay_hbm, back_hbm, chan_hbm, pack_hbm, unpack_hbm,
     cot_hbm, table_hbm,
-    llm_out, got_out, row_ref,
+    llm_out, got_out, gpre_out, row_ref,
     ids_ref, pos_ref, frames, cw, wown, relay, backm, chan, pack, unpack,
     cot, table, sel_s, f_a, f_b, f_c, f_d, r_a, r_b, r_c, r_d,
     idsnd, idrcv, idcomp, idall, halo, ext, cwf, act, pooled, plo, plp,
-    wpadf, wpk, wrz, wst, wfull, xs, far, opp, text, llm, passing,
+    wpadf, wpk, wrz, wst, wfull, xs, far, opp, text, llm, passing, place, gpre,
     loc_sem, halo_sem, idz_sem, idp_sem, wz_sem,
     f1_sem, f2_sem, r1_sem, r2_sem,
     ws_sem, w1_sem, wr_sem, wl_sem, pool_s, pool_r, xx_sem, xo_sem,
@@ -351,28 +352,31 @@
     mine = lax.rem(x, 2)
     wfull[pl.ds(prow80, KB), :] = wst[mine]
 
-    def wblock(f, g):
-        return wfull.at[pl.ds(pl.multiple_of((lax.rem(x + f, 4) * 4 + lax.rem(y + g, 4)) * KB, 16), KB)]
+    def wblock(f, g, cols=WHOLE):
+        row = pl.multiple_of((lax.rem(x + f, 4) * 4 + lax.rem(y + g, 4)) * KB, 16)
+        return wfull.at[pl.ds(row, KB), pl.ds(cols[0], cols[1])]
 
     def wsend(block, dst, sem, dev):
         remote(block, dst, ws_sem.at[0], sem, dev).start()
 
-    def wsecond(f):
-        up, down = (wr_sem.at[f], wl_sem.at[0]) if f < 2 else (wl_sem.at[0], wr_sem.at[f])
-        wsend(wblock(f, 0), wblock(f, 0), up, at(x, z, lax.rem(y + 1, 4)))
-        wsend(wblock(f, 0), wblock(f, 0), down, at(x, z, lax.rem(y + 3, 4)))
-
-    def w2relay(f):
+    def wsecond(f, part):
+        passed, ends = wr_sem.at[part[2], f], wl_sem.at[part[2]]
+        up, down = (passed, ends) if f < 2 else (ends, passed)
+        wsend(wblock(f, 0, part), wblock(f, 0, part), up, at(x, z, lax.rem(y + 1, 4)))
+        wsend(wblock(f, 0, part), wblock(f, 0, part), down, at(x, z, lax.rem(y + 3, 4)))
+
+    def w2relay(f, part):
         near, to = (3, 1) if f < 2 else (1, 3)
-        wait_got(wblock(f, near), wr_sem.at[f])
-        wsend(wblock(f, near), wblock(f, near), wl_sem.at[0], at(x, z, lax.rem(y + to, 4)))
+        wait_got(wblock(f, near, part), wr_sem.at[part[2], f])
+        wsend(wblock(f, near, part), wblock(f, near, part), wl_sem.at[part[2]], at(x, z, lax.rem(y + to, 4)))
 
     def xpeer(f):
         return at(lax.rem(x + f, 4), z, y)
 
     for f in (1, 3, 2):
         wsend(wst.at[mine if f == 2 else 1 - mine], wblock(0, 0), w1_sem.at[f], xpeer(f))
-    wsecond(0)
+    for part in EARLY:
+        wsecond(0, part)
 
     wait_all(idall.at[pl.ds(0, 120)], idp_sem.at[0], idp_sem.at[1])
     dup = []
@@ -423,13 +427,16 @@
     turn(f_b, f_c, f_d, f1_sem.at[0], f2_sem, 1)
     for f in (1, 3, 2):
         wait_got(wblock(f, 0), w1_sem.at[4 - f])
-        wsecond(f)
+        wsecond(f, EARLY[0])
+    for f in (1, 3, 2):
+        wsecond(f, EARLY[1])
 
     turn(r_b, r_c, r_d, r1_sem, r2_sem, 0)
     next_cp.wait()
     fwd_cp = remote(plp.at[v], plp.at[v], pool_s.at[2], pool_r.at[2], other)
     fwd_cp.start()
-    w2relay(0)
+    for part in EARLY:
+        w2relay(0, part)
 
     core_cp.wait()
     fwd_cp.wait()
@@ -446,8 +453,9 @@
     xsend(xs.at[v, pl.ds(RUN, RUN)], xs.at[v, pl.ds(SLOT + RUN, RUN)], xx_sem, 3)
 
     turn(r_b, r_c, r_d, r1_sem, r2_sem, 1)
-    for f in (1, 3, 2):
-        w2relay(f)
+    for part in EARLY:
+        for f in (1, 3, 2):
+            w2relay(f, part)
 
     wait_all(xs.at[v, pl.ds(SLOT, SLOT)], xx_sem.at[0], xx_sem.at[1])
     x_cp = remote(xs.at[v, pl.ds(SLOT, SLOT)], xs.at[v, pl.ds(SLOT, SLOT)], pool_s.at[3], pool_r.at[3], other)
@@ -461,19 +469,33 @@
         got_cps.append(pltpu.make_async_copy(f_c.at[c], got_out.at[:, pl.ds(c * CW, CW)], loc_sem.at[2 + c]))
         got_cps[-1].start()
     row_ref[...] = jnp.broadcast_to(rowrow, (8, SLOT))
+    vrow = lax.broadcasted_iota(jnp.int32, (VROWS, SLOT), 0)
+    place[...] = jnp.where(vrow == rowrow, 1.0, 0.0).astype(BF)
+
+    def gtile(i, carry):
+        cols = pl.ds(pl.multiple_of(i * TILE, TILE), TILE)
+        gpre[:, cols] = mm(place[...], f_c[0, :, cols]).astype(BF)
+        return carry
+
+    lax.fori_loop(0, PRE, gtile, 0)
+    got_cps.append(pltpu.make_async_copy(gpre, gpre_out, loc_sem.at[4]))
+    got_cps[-1].start()
     x_cp.wait()
-    wait_got(wfull.at[pl.ds(0, 8 * KB)], wl_sem.at[0])
-    far[...] = (mm(xs[0, SLOT:, :], wfull[0:CH, :]) + mm(xs[1, SLOT:, :], wfull[CH:, :])).astype(BF)
-    xsend(far.at[pl.ds(0, RUN)], opp.at[pl.ds(0, RUN)], xo_sem, 3)
-    xsend(far.at[pl.ds(RUN, RUN)], opp.at[pl.ds(RUN, RUN)], xo_sem, 1)
-    near = mm(xs[0, 0:SLOT, :], wfull[0:CH, :]) + mm(xs[1, 0:SLOT, :], wfull[CH:, :])
-    near = near.astype(BF).astype(F32)
+    for part in EARLY:
+        cols = pl.ds(part[0], part[1])
+        wait_got(wfull.at[pl.ds(0, 8 * KB), cols], wl_sem.at[part[2]])
+        far[:, cols] = (mm(xs[0, SLOT:, :], wfull[0:CH, cols]) + mm(xs[1, SLOT:, :], wfull[CH:, cols])).astype(BF)
+        xsend(far.at[pl.ds(0, RUN), cols], opp.at[pl.ds(0, RUN), cols], xo_sem, 3)
+        xsend(far.at[pl.ds(RUN, RUN), cols], opp.at[pl.ds(RUN, RUN), cols], xo_sem, 1)
+        llm[mine, :, cols] = (
+            mm(xs[0, 0:SLOT, :], wfull[0:CH, cols]) + mm(xs[1, 0:SLOT, :], wfull[CH:, cols])
+        ).astype(BF)
     for c in range(NC):
         z_wait(r_d, r2_sem, c)
         text[c] = lax.dot_general(
             sel_s[...], r_d[c], (((0,), (0,)), ((), ())), preferred_element_type=F32
         ).astype(BF)
-    llm[mine] = (near + text[mine].astype(F32)).astype(BF)
+    llm[mine] = (llm[mine].astype(F32) + text[mine].astype(F32)).astype(BF)
     outs = [pltpu.make_async_copy(llm.at[mine], llm_out.at[mine], loc_sem.at[0])]
     outs[0].start()
     wait_all(opp, xo_sem.at[0], xo_sem.at[1])
@@ -492,7 +514,9 @@
         cp.wait()
 
 
-def write_kernel(row_hbm, got_hbm, llm_hbm, out_hbm, grad_hbm, row, got, llm, grad, place, in_sem, out_sem):
+def write_kernel(
+    row_hbm, got_hbm, llm_hbm, ready_hbm, out_hbm, grad_hbm, row, got, llm, ready, grad, place, in_sem, out_sem
+):
     tiles = D // TILE
 
     def get(i):
@@ -509,8 +533,11 @@
     row_cp = pltpu.make_async_copy(row_hbm, row, in_sem.at[tiles])
     row_cp.start()
     llm_in = pltpu.make_async_copy(llm_hbm, llm, in_sem.at[tiles + 1])
-    for i in range(tiles):
+    for i in range(PRE, tiles):
         get(i).start()
+    ready_in = pltpu.make_async_copy(ready_hbm, ready, in_sem.at[0])
+    ready_in.start()
+    ready_out = pltpu.make_async_copy(ready, grad_hbm.at[:, pl.ds(0, PRE * TILE)], out_sem.at[0])
     llm_in.start()
     row_cp.wait()
     vi = lax.broadcasted_iota(jnp.int32, (VROWS, SLOT), 0)
@@ -522,12 +549,16 @@
         put(i).start()
         return c
 
-    lax.fori_loop(0, tiles, tile, 0)
+    lax.fori_loop(PRE, PRE + 1, tile, 0)
+    ready_in.wait()
+    ready_out.start()
+    lax.fori_loop(PRE + 1, tiles, tile, 0)
     llm_in.wait()
     for h in range(NC):
         put_llm(h).start()
-    for i in range(tiles):
+    for i in range(PRE, tiles):
         put(i).wait()
+    ready_out.wait()
     for h in range(NC):
         put_llm(h).wait()
 
@@ -540,15 +571,16 @@
     anywhere = pl.BlockSpec(memory_space=pl.ANY)
     dma = pltpu.SemaphoreType.DMA
     wide = pltpu.VMEM((NC, SLOT, CW), BF)
-    llm, got, rows = pl.pallas_call(
+    llm, got, ready, rows = pl.pallas_call(
         comm_kernel,
         out_shape=[
             jax.ShapeDtypeStruct((NC, SLOT, CW), BF),
             jax.ShapeDtypeStruct((SLOT, D), BF),
+            jax.ShapeDtypeStruct((VROWS, PRE * TILE), BF),
             jax.ShapeDtypeStruct((8, SLOT), jnp.int32),
         ],
         in_specs=[hbm] * 12,
-        out_specs=[anywhere, anywhere, pl.BlockSpec(memory_space=pltpu.VMEM)],
+        out_specs=[anywhere, anywhere, anywhere, pl.BlockSpec(memory_space=pltpu.VMEM)],
         scratch_shapes=[
             pltpu.VMEM((1, SLOT), jnp.int32),
             pltpu.VMEM((1, RUN), jnp.int32),
@@ -585,9 +617,11 @@
             pltpu.VMEM((SLOT, CW), BF),
             wide, wide,
             pltpu.VMEM((PART, CH), BF),
+            pltpu.VMEM((VROWS, SLOT), BF),
+            pltpu.VMEM((VROWS, PRE * TILE), BF),
             dma((12,)), dma((2,)), dma((2,)), dma((2,)), dma((7,)),
             dma((2, 2, 2)), dma((2, 2)), dma((2, 2)), dma((2, 2)),
-            dma((1,)), dma((4,)), dma((4,)), dma((1,)), dma((5,)), dma((5,)), dma((2,)), dma((2,)),
+            dma((1,)), dma((4,)), dma((2, 4)), dma((2,)), dma((5,)), dma((5,)), dma((2,)), dma((2,)),
         ],
         compiler_params=pltpu.CompilerParams(
             collective_id=0, has_side_effects=True, vmem_limit_bytes=VMEM_LIMIT
@@ -600,12 +634,13 @@
     return pl.pallas_call(
         write_kernel,
         out_shape=[jax.ShapeDtypeStruct((SLOT, D), BF), jax.ShapeDtypeStruct((VROWS, D), BF)],
-        in_specs=[hbm] * 3,
+        in_specs=[hbm] * 4,
         out_specs=[anywhere, anywhere],
         scratch_shapes=[
             pltpu.VMEM((8, SLOT), jnp.int32),
             pltpu.VMEM((D // TILE, SLOT, TILE), BF),
             wide,
+            pltpu.VMEM((VROWS, PRE * TILE), BF),
             pltpu.VMEM((D // TILE, VROWS, TILE), BF),
             pltpu.VMEM((VROWS, SLOT), BF),
             dma((D // TILE + 2,)),
@@ -613,7 +648,7 @@
         ],
         compiler_params=pltpu.CompilerParams(vmem_limit_bytes=VMEM_LIMIT),
         name="write",
-    )(rows, got, llm)
+    )(rows, got, llm, ready)
 
 
 def solution(mesh):

time: 69.6 us -> 67.7 us (0.973)
  Pallas kernels: 67.7 us -> 66 us
    pallas_call x1, Pallas kernels: 63.3 us -> 61.9 us  [shards(): pl.pallas_call(comm_kernel, out_shape=[jax.ShapeDtypeStruct((NC, SLOT, CW...]
where the time goes in v4:
time: 67.7 us; the launch traced here: 66.6 us
  Pallas kernels  66 us (97%)
    pallas_call x1, Pallas kernels, shards(): pl.pallas_call(comm_kernel, out_shape=[jax.ShapeDtypeStruct((NC, SLOT, CW...  61.9 us
    pallas_call x1, Pallas kernels, shards(): pl.pallas_call(write_kernel, out_shape=[jax.ShapeDtypeStruct((SLOT, D), B...  4.07 us

profile of v4, /device:TPU:2, one launch (start us, length us, event | category | flops | bytes accessed | tf_op | source)
XLA Modules:
  0.0 66.6 jit_solution(2369987749870938605)
XLA Ops:
  0.6 61.9 %exchange.1 = (bf16[2,256,896]{2,1,0:T(8,128)(2,1)}, bf16[256,1792]{1,0:T(8,128)(2,1)}, bf16[1188,768]{1,0:T(8,128)(2,1)}, s32[8,256]{1,0:T(8,128)}) custom-call(s32[1,256]{1,0:T(1,128)} %bitcast.2, s32[1,128]{1,0:T(1,128)} %bitcast.3, bf16[512,640]{1,0:T(8,128)(2,1)} %frames_hbm.1, bf16[31,640]{1,0:T(8,128)(2,1)} %cw_hbm.1, bf16[10,1792]{1,0:T(8,128)(2,1)} %w_hbm.1, ...), custom_call_target="tpu_custom_call" | custom-call | tf_op jit(solution)/shard_map/exchange/pallas_call | solution.py:574
  62.5 4.1 %write.1 = (bf16[256,1792]{1,0:T(8,128)(2,1)}, bf16[1188,1792]{1,0:T(8,128)(2,1)}) custom-call(s32[8,256]{1,0:T(8,128)} %get-tuple-element.6.row_hbm, bf16[256,1792]{1,0:T(8,128)(2,1)} %get-tuple-element.7.got_hbm, bf16[2,256,896]{2,1,0:T(8,128)(2,1)} %get-tuple-element.8.llm_hbm, bf16[1188,768]{1,0:T(8,128)(2,1)} %get-tuple-element.9.ready_hbm), custom_call_target="tpu_custom_call" | custom-call | tf_op jit(solution)/shard_map/write/pallas_call | solution.py:634

commit v5 on v4

--- a/solution.py
+++ b/solution.py
@@ -31,7 +31,7 @@
 WP = 1152
 KB = NZ * WROWS
 TILE = 256
-PRE = 3
+PRE = 5
 VMEM_LIMIT = 60 * 1024 * 1024
 
 
@@ -88,7 +88,7 @@
     ids_ref, pos_ref, frames, cw, wown, relay, backm, chan, pack, unpack,
     cot, table, sel_s, f_a, f_b, f_c, f_d, r_a, r_b, r_c, r_d,
     idsnd, idrcv, idcomp, idall, halo, ext, cwf, act, pooled, plo, plp,
-    wpadf, wpk, wrz, wst, wfull, xs, far, opp, text, llm, passing, place, gpre,
+    wpadf, wpk, wrz, wst, wfull, xs, far, opp, text, llm, passing, place, gpre, gotv,
     loc_sem, halo_sem, idz_sem, idp_sem, wz_sem,
     f1_sem, f2_sem, r1_sem, r2_sem,
     ws_sem, w1_sem, wr_sem, wl_sem, pool_s, pool_r, xx_sem, xo_sem,
@@ -176,7 +176,7 @@
         z_send(mid, last, sem2, c, part)
 
     bar = pltpu.get_barrier_semaphore()
-    for d in range(1, 8):
+    for d in (4, 3, 5, 2, 6, 1, 7):
         pl.semaphore_signal(bar, inc=1, device_id=zpeer(d), device_id_type=MESH)
     plane(lambda j: pl.semaphore_signal(bar, inc=1, device_id=ppeer(j), device_id_type=MESH))
     for dev in (nxt, prv, other, ahead):
@@ -314,10 +314,11 @@
         ).astype(BF)
         return carry
 
-    lax.fori_loop(0, 20, conv, 0)
-
-    for part in EARLY:
-        turn(f_b, f_c, f_d, f1_sem.at[part[2]], f2_sem, 0, part)
+    lax.fori_loop(0, 10, conv, 0)
+
+    turn(f_b, f_c, f_d, f1_sem.at[0], f2_sem, 0, EARLY[0])
+    lax.fori_loop(10, 20, conv, 0)
+    turn(f_b, f_c, f_d, f1_sem.at[1], f2_sem, 0, EARLY[1])
     lax.fori_loop(20, 40, conv, 0)
     plo[v] = mm(pooled[...], chan[...]).astype(BF)
     core_cp = remote(plo.at[v], plo.at[v], pool_s.at[0], pool_r.at[0], other)
@@ -335,48 +336,6 @@
         for i in range(3):
             remote(plo.at[v, pl.ds(i * PART, PART)], passing, pool_s.at[1], pool_r.at[4], at(x, z, i)).start()
 
-
-    wait_got(wrz.at[pl.ds(0, 80)], wz_sem.at[1])
-    sent = wrz.at[pl.ds(0, 112)]
-    remote(sent, sent, wz_sem.at[0], wz_sem.at[1], other).wait_send()
-    prow80 = pl.multiple_of(p * KB, 16)
-    packed = wrz[...]
-    for c in range(NC):
-        wst[c, 0:64, :] = mm(unpack[64 * c : 64 * c + 64], packed[:, 0:half]).astype(BF)
-    for g in range(7):
-        piece = mm(unpack[128 + 16 * g : 144 + 16 * g], packed[:, half:]).astype(BF)
-        for b in range(2):
-            col = 256 * g + 128 * b
-            c, off = col // CW, col % CW
-            wst[c, 64:KB, off : off + 128] = piece[:, 128 * b : 128 * b + 128]
-    mine = lax.rem(x, 2)
-    wfull[pl.ds(prow80, KB), :] = wst[mine]
-
-    def wblock(f, g, cols=WHOLE):
-        row = pl.multiple_of((lax.rem(x + f, 4) * 4 + lax.rem(y + g, 4)) * KB, 16)
-        return wfull.at[pl.ds(row, KB), pl.ds(cols[0], cols[1])]
-
-    def wsend(block, dst, sem, dev):
-        remote(block, dst, ws_sem.at[0], sem, dev).start()
-
-    def wsecond(f, part):
-        passed, ends = wr_sem.at[part[2], f], wl_sem.at[part[2]]
-        up, down = (passed, ends) if f < 2 else (ends, passed)
-        wsend(wblock(f, 0, part), wblock(f, 0, part), up, at(x, z, lax.rem(y + 1, 4)))
-        wsend(wblock(f, 0, part), wblock(f, 0, part), down, at(x, z, lax.rem(y + 3, 4)))
-
-    def w2relay(f, part):
-        near, to = (3, 1) if f < 2 else (1, 3)
-        wait_got(wblock(f, near, part), wr_sem.at[part[2], f])
-        wsend(wblock(f, near, part), wblock(f, near, part), wl_sem.at[part[2]], at(x, z, lax.rem(y + to, 4)))
-
-    def xpeer(f):
-        return at(lax.rem(x + f, 4), z, y)
-
-    for f in (1, 3, 2):
-        wsend(wst.at[mine if f == 2 else 1 - mine], wblock(0, 0), w1_sem.at[f], xpeer(f))
-    for part in EARLY:
-        wsecond(0, part)
 
     wait_all(idall.at[pl.ds(0, 120)], idp_sem.at[0], idp_sem.at[1])
     dup = []
@@ -406,8 +365,10 @@
     vi = lax.broadcasted_iota(jnp.int32, (SLOT, VROWS), 1)
     look = jnp.where(vi == rowid, 1.0, 0.0).astype(BF)
 
-    r_a[0] = mm(look, table[:, 0:CW]).astype(BF)
-    p_send(r_a, r_b, r1_sem, 0)
+    for part in EARLY:
+        cols = pl.ds(part[0], part[1])
+        r_a[0, :, cols] = mm(look, table[:, cols]).astype(BF)
+        p_send(r_a, r_b, r1_sem.at[part[2]], 0, part)
     r_a[1] = mm(look, table[:, CW:]).astype(BF)
 
     rowrow = jnp.sum(jnp.where(diag, rowid.astype(F32), 0.0), axis=0, keepdims=True).astype(jnp.int32)
@@ -417,7 +378,49 @@
     before = jnp.sum(jnp.where(mlane == mprev, strow, 0.0), axis=1, keepdims=True).astype(jnp.int32)
     before = jnp.where(s > 0, before, -4096)
 
-    p_send(r_a, r_b, r1_sem, 1)
+    wait_got(wrz.at[pl.ds(0, 80)], wz_sem.at[1])
+    sent = wrz.at[pl.ds(0, 112)]
+    remote(sent, sent, wz_sem.at[0], wz_sem.at[1], other).wait_send()
+    prow80 = pl.multiple_of(p * KB, 16)
+    packed = wrz[...]
+    for c in range(NC):
+        wst[c, 0:64, :] = mm(unpack[64 * c : 64 * c + 64], packed[:, 0:half]).astype(BF)
+    for g in range(7):
+        piece = mm(unpack[128 + 16 * g : 144 + 16 * g], packed[:, half:]).astype(BF)
+        for b in range(2):
+            col = 256 * g + 128 * b
+            c, off = col // CW, col % CW
+            wst[c, 64:KB, off : off + 128] = piece[:, 128 * b : 128 * b + 128]
+    mine = lax.rem(x, 2)
+    wfull[pl.ds(prow80, KB), :] = wst[mine]
+
+    def wblock(f, g, cols=WHOLE):
+        row = pl.multiple_of((lax.rem(x + f, 4) * 4 + lax.rem(y + g, 4)) * KB, 16)
+        return wfull.at[pl.ds(row, KB), pl.ds(cols[0], cols[1])]
+
+    def wsend(block, dst, sem, dev):
+        remote(block, dst, ws_sem.at[0], sem, dev).start()
+
+    def wsecond(f, part):
+        passed, ends = wr_sem.at[part[2], f], wl_sem.at[part[2]]
+        up, down = (passed, ends) if f < 2 else (ends, passed)
+        wsend(wblock(f, 0, part), wblock(f, 0, part), up, at(x, z, lax.rem(y + 1, 4)))
+        wsend(wblock(f, 0, part), wblock(f, 0, part), down, at(x, z, lax.rem(y + 3, 4)))
+
+    def w2relay(f, part):
+        near, to = (3, 1) if f < 2 else (1, 3)
+        wait_got(wblock(f, near, part), wr_sem.at[part[2], f])
+        wsend(wblock(f, near, part), wblock(f, near, part), wl_sem.at[part[2]], at(x, z, lax.rem(y + to, 4)))
+
+    def xpeer(f):
+        return at(lax.rem(x + f, 4), z, y)
+
+    for f in (1, 3, 2):
+        wsend(wst.at[mine if f == 2 else 1 - mine], wblock(0, 0), w1_sem.at[f], xpeer(f))
+    for part in EARLY:
+        wsecond(0, part)
+
+    p_send(r_a, r_b, r1_sem.at[0], 1)
     @pl.when(y < 3)
     def _():
         part = pl.ds(pl.multiple_of(y * PART, PART), PART)
@@ -431,7 +434,8 @@
     for f in (1, 3, 2):
         wsecond(f, EARLY[1])
 
-    turn(r_b, r_c, r_d, r1_sem, r2_sem, 0)
+    for part in EARLY:
+        turn(r_b, r_c, r_d, r1_sem.at[part[2]], r2_sem, 0, part)
     next_cp.wait()
     fwd_cp = remote(plp.at[v], plp.at[v], pool_s.at[2], pool_r.at[2], other)
     fwd_cp.start()
@@ -452,7 +456,7 @@
     xsend(xs.at[v, pl.ds(0, RUN)], xs.at[v, pl.ds(SLOT, RUN)], xx_sem, 1)
     xsend(xs.at[v, pl.ds(RUN, RUN)], xs.at[v, pl.ds(SLOT + RUN, RUN)], xx_sem, 3)
 
-    turn(r_b, r_c, r_d, r1_sem, r2_sem, 1)
+    turn(r_b, r_c, r_d, r1_sem.at[0], r2_sem, 1)
     for part in EARLY:
         for f in (1, 3, 2):
             w2relay(f, part)
@@ -465,16 +469,16 @@
         z_wait(f_d, f2_sem, c)
     got_cps = []
     for c in range(NC):
-        f_c[c] = mm(relay[...], f_d[c]).astype(BF)
-        got_cps.append(pltpu.make_async_copy(f_c.at[c], got_out.at[:, pl.ds(c * CW, CW)], loc_sem.at[2 + c]))
-        got_cps[-1].start()
+        gotv[:, c * CW : (c + 1) * CW] = mm(relay[...], f_d[c]).astype(BF)
+    got_cps.append(pltpu.make_async_copy(gotv, got_out, loc_sem.at[2]))
+    got_cps[-1].start()
     row_ref[...] = jnp.broadcast_to(rowrow, (8, SLOT))
     vrow = lax.broadcasted_iota(jnp.int32, (VROWS, SLOT), 0)
     place[...] = jnp.where(vrow == rowrow, 1.0, 0.0).astype(BF)
 
     def gtile(i, carry):
         cols = pl.ds(pl.multiple_of(i * TILE, TILE), TILE)
-        gpre[:, cols] = mm(place[...], f_c[0, :, cols]).astype(BF)
+        gpre[i] = mm(place[...], gotv[:, cols]).astype(BF)
         return carry
 
     lax.fori_loop(0, PRE, gtile, 0)
@@ -515,7 +519,7 @@
 
 
 def write_kernel(
-    row_hbm, got_hbm, llm_hbm, ready_hbm, out_hbm, grad_hbm, row, got, llm, ready, grad, place, in_sem, out_sem
+    row_hbm, got_hbm, llm_hbm, ready_hbm, out_hbm, grad_hbm, row, got, llm, grad, place, in_sem, out_sem
 ):
     tiles = D // TILE
 
@@ -535,9 +539,9 @@
     llm_in = pltpu.make_async_copy(llm_hbm, llm, in_sem.at[tiles + 1])
     for i in range(PRE, tiles):
         get(i).start()
-    ready_in = pltpu.make_async_copy(ready_hbm, ready, in_sem.at[0])
-    ready_in.start()
-    ready_out = pltpu.make_async_copy(ready, grad_hbm.at[:, pl.ds(0, PRE * TILE)], out_sem.at[0])
+    ready = [pltpu.make_async_copy(ready_hbm.at[i], grad.at[i], in_sem.at[i]) for i in range(PRE)]
+    for cp in ready:
+        cp.start()
     llm_in.start()
     row_cp.wait()
     vi = lax.broadcasted_iota(jnp.int32, (VROWS, SLOT), 0)
@@ -549,16 +553,15 @@
         put(i).start()
         return c
 
-    lax.fori_loop(PRE, PRE + 1, tile, 0)
-    ready_in.wait()
-    ready_out.start()
-    lax.fori_loop(PRE + 1, tiles, tile, 0)
+    lax.fori_loop(PRE, tiles, tile, 0)
+    for i in range(PRE):
+        ready[i].wait()
+        put(i).start()
     llm_in.wait()
     for h in range(NC):
         put_llm(h).start()
-    for i in range(PRE, tiles):
+    for i in range(tiles):
         put(i).wait()
-    ready_out.wait()
     for h in range(NC):
         put_llm(h).wait()
 
@@ -576,7 +579,7 @@
         out_shape=[
             jax.ShapeDtypeStruct((NC, SLOT, CW), BF),
             jax.ShapeDtypeStruct((SLOT, D), BF),
-            jax.ShapeDtypeStruct((VROWS, PRE * TILE), BF),
+            jax.ShapeDtypeStruct((PRE, VROWS, TILE), BF),
             jax.ShapeDtypeStruct((8, SLOT), jnp.int32),
         ],
         in_specs=[hbm] * 12,
@@ -618,9 +621,10 @@
             wide, wide,
             pltpu.VMEM((PART, CH), BF),
             pltpu.VMEM((VROWS, SLOT), BF),
-            pltpu.VMEM((VROWS, PRE * TILE), BF),
+            pltpu.VMEM((PRE, VROWS, TILE), BF),
+            pltpu.VMEM((SLOT, D), BF),
             dma((12,)), dma((2,)), dma((2,)), dma((2,)), dma((7,)),
-            dma((2, 2, 2)), dma((2, 2)), dma((2, 2)), dma((2, 2)),
+            dma((2, 2, 2)), dma((2, 2)), dma((2, 2, 2)), dma((2, 2)),
             dma((1,)), dma((4,)), dma((2, 4)), dma((2,)), dma((5,)), dma((5,)), dma((2,)), dma((2,)),
         ],
         compiler_params=pltpu.CompilerParams(
@@ -640,7 +644,6 @@
             pltpu.VMEM((8, SLOT), jnp.int32),
             pltpu.VMEM((D // TILE, SLOT, TILE), BF),
             wide,
-            pltpu.VMEM((VROWS, PRE * TILE), BF),
             pltpu.VMEM((D // TILE, VROWS, TILE), BF),
             pltpu.VMEM((VROWS, SLOT), BF),
             dma((D // TILE + 2,)),

time: 67.7 us -> 67.3 us (level); the launches traced: 66.6 us -> 67.1 us
    pallas_call x1, Pallas kernels: 61.9 us -> 62.6 us  [shards(): pl.pallas_call(comm_kernel, out_shape=[jax.ShapeDtypeStruct((NC, SLOT, CW...]
where the time goes in v5:
time: 67.3 us; the launch traced here: 67.1 us
  Pallas kernels  66.5 us (99%)
    pallas_call x1, Pallas kernels, shards(): pl.pallas_call(comm_kernel, out_shape=[jax.ShapeDtypeStruct((NC, SLOT, CW...  62.6 us
    pallas_call x1, Pallas kernels, shards(): pl.pallas_call(write_kernel, out_shape=[jax.ShapeDtypeStruct((SLOT, D), B...  3.84 us

profile of v5, /device:TPU:2, one launch (start us, length us, event | category | flops | bytes accessed | tf_op | source)
XLA Modules:
  0.0 67.1 jit_solution(18267747819218214767)
XLA Ops:
  0.6 62.6 %exchange.1 = (bf16[2,256,896]{2,1,0:T(8,128)(2,1)}, bf16[256,1792]{1,0:T(8,128)(2,1)}, bf16[5,1188,256]{2,1,0:T(8,128)(2,1)}, s32[8,256]{1,0:T(8,128)}) custom-call(s32[1,256]{1,0:T(1,128)} %bitcast.2, s32[1,128]{1,0:T(1,128)} %bitcast.3, bf16[512,640]{1,0:T(8,128)(2,1)} %frames_hbm.1, bf16[31,640]{1,0:T(8,128)(2,1)} %cw_hbm.1, bf16[10,1792]{1,0:T(8,128)(2,1)} %w_hbm.1, ...), custom_call_target="tpu_custom_call" | custom-call | tf_op jit(solution)/shard_map/exchange/pallas_call | solution.py:577
  63.3 3.8 %write.1 = (bf16[256,1792]{1,0:T(8,128)(2,1)}, bf16[1188,1792]{1,0:T(8,128)(2,1)}) custom-call(s32[8,256]{1,0:T(8,128)} %get-tuple-element.6.row_hbm, bf16[256,1792]{1,0:T(8,128)(2,1)} %get-tuple-element.7.got_hbm, bf16[2,256,896]{2,1,0:T(8,128)(2,1)} %get-tuple-element.8.llm_hbm, bf16[5,1188,256]{2,1,0:T(8,128)(2,1)} %get-tuple-element.9.ready_hbm), custom_call_target="tpu_custom_call" | custom-call | tf_op jit(solution)/shard_map/write/pallas_call | solution.py:638
